TPU v7x, 256 devices: a whole 4x4x8 slice. The times are simulated.
256 devices in a mesh: grp: 2 (over core), ep: 128 (over z, y, x).
Axes of the slice: x: 4, y: 4, z: 8, core: 2. Of those that a mesh axis runs over, the one named last changes fastest.
Arguments:
- activations: bfloat16 [32768, 2048], P(('grp', 'ep')), may hold values from -6 to 6
- out_grad: bfloat16 [32768, 2048], P(('grp', 'ep')), may hold values from -6 to 6
- expert_ids: int32 [32768, 4], P(('grp', 'ep')), may hold values from 0 to 127, all different within a row; in each aligned block of 128 rows (0 to 127, 128 to 255, ...) at most 5 rows name the same one
- gate_values: bfloat16 [32768, 4], P(('grp', 'ep')), may hold values from 0.049804688 to 1
- w_gate: bfloat16 [128, 2048, 768], P('ep', None, 'grp'), may hold values from -0.125 to 0.125
- w_up: bfloat16 [128, 2048, 768], P('ep', None, 'grp'), may hold values from -0.125 to 0.125
- w_down: bfloat16 [128, 768, 2048], P('ep', 'grp'), may hold values from -0.21875 to 0.21875
Outputs:
- grad_input: bfloat16 [32768, 2048], P(('grp', 'ep'))
- grad_gate: bfloat16 [128, 2048, 768], P('ep', None, 'grp')
- grad_up: bfloat16 [128, 2048, 768], P('ep', None, 'grp')
- grad_down: bfloat16 [128, 768, 2048], P('ep', 'grp')
Inputs may be any that keep to these rules, and one draw needn't show every extreme that they name: `expert_ids`: each token names 4 different experts. Among the 128 tokens of one device no expert is named by more than 5 pairs, a bound that some block reaches.
All inputs are finite; a program needn't handle non-finite values.
Results may differ from a plain program's by a relative error of at most 0.012.
Values may be sent and summed in bfloat16 or wider, within the bound.
No kernel may reach another device: no remote copies, remote signals or barrier semaphores. Data moves between devices by JAX's collectives and lax.ppermute only.
A program may use at most 192 MiB of HBM per device.

v0:
```python
import math

import jax
import jax.numpy as jnp
from jax import lax
from jax.sharding import PartitionSpec as P


def routing_table(expert_ids, experts, capacity):
    flattened = expert_ids.reshape(-1)
    pair_total = flattened.shape[0]
    block_rows = math.gcd(pair_total, 512)
    block_count = pair_total // block_rows
    onehot = (flattened[:, None] == jnp.arange(experts, dtype=jnp.int32)[None, :]).astype(
        jnp.bfloat16
    )
    stacked = onehot.reshape(block_count, block_rows, experts)
    row_ids = jnp.arange(block_rows, dtype=jnp.int32)
    lower_mask = (row_ids[:, None] > row_ids[None, :]).astype(jnp.bfloat16)
    within = jnp.einsum("ij,bjk->bik", lower_mask, stacked, preferred_element_type=jnp.float32)
    totals = jnp.sum(stacked.astype(jnp.float32), axis=1)
    before = jnp.cumsum(totals, axis=0) - totals
    earlier = (within + before[:, None, :]).reshape(pair_total, experts)
    slot_index = jnp.sum(earlier * onehot.astype(jnp.float32), axis=1).astype(jnp.int32)
    source_table = jnp.full((experts, capacity), -1, jnp.int32)
    source_table = source_table.at[flattened, slot_index].set(
        jnp.arange(pair_total, dtype=jnp.int32)
    )
    return (slot_index, source_table)


def contract_rows(left, right):
    return lax.dot_general(
        left, right, (((0,), (0,)), ((), ())), preferred_element_type=jnp.float32
    )


def contract_last(left, right):
    return lax.dot_general(
        left, right, (((1,), (1,)), ((), ())), preferred_element_type=jnp.float32
    )


def expert_backward(token_rows, upstream_rows, gate_rows, gate_weight, up_weight, down_weight):
    pre_gate = jnp.dot(token_rows, gate_weight, preferred_element_type=jnp.float32)
    pre_up = jnp.dot(token_rows, up_weight, preferred_element_type=jnp.float32)
    sigmoid_gate = jax.nn.sigmoid(pre_gate)
    silu_gate = pre_gate * sigmoid_gate
    row_scale = gate_rows.astype(jnp.float32)[:, None]
    weighted = (row_scale * silu_gate * pre_up).astype(jnp.bfloat16)
    grad_down = contract_rows(weighted, upstream_rows)
    grad_hidden = row_scale * contract_last(upstream_rows, down_weight)
    grad_pre_gate = (
        grad_hidden * pre_up * sigmoid_gate * (1.0 + pre_gate * (1.0 - sigmoid_gate))
    ).astype(jnp.bfloat16)
    grad_pre_up = (grad_hidden * silu_gate).astype(jnp.bfloat16)
    grad_gate = contract_rows(token_rows, grad_pre_gate)
    grad_up = contract_rows(token_rows, grad_pre_up)
    return (grad_pre_gate, grad_pre_up, grad_gate, grad_up, grad_down)


def input_rows(grad_pre_gate, grad_pre_up, gate_weight, up_weight):
    return contract_last(grad_pre_gate, gate_weight) + contract_last(grad_pre_up, up_weight)


def dispatch_rows(activations, out_grad, gate_values, source_table, top_count):
    occupied = source_table >= 0
    safe_index = jnp.where(occupied, source_table, 0)
    token_index = safe_index // top_count
    zero_value = jnp.zeros((), jnp.bfloat16)
    send_tokens = jnp.where(occupied[:, :, None], activations[token_index], zero_value)
    send_upstream = jnp.where(occupied[:, :, None], out_grad[token_index], zero_value)
    send_gates = jnp.where(occupied, gate_values.reshape(-1)[safe_index], zero_value)
    return (send_tokens, send_upstream, send_gates)


def local(activations, out_grad, expert_ids, gate_values, w_gate, w_up, w_down):
    experts = lax.axis_size("ep") * w_gate.shape[0]
    tok_count, top_count = expert_ids.shape
    model_width = activations.shape[1]
    capacity = max(2, 5 * tok_count * top_count // (4 * experts))
    slot_index, source_table = routing_table(expert_ids, experts, capacity)
    send_tokens, send_upstream, send_gates = dispatch_rows(
        activations, out_grad, gate_values, source_table, top_count
    )
    gate_half, up_half, down_half = (w_gate[0], w_up[0], w_down[0])
    arrived_tokens, arrived_upstream, arrived_gates = (
        lax.all_to_all(send_tokens, "ep", split_axis=0, concat_axis=0, tiled=True),
        lax.all_to_all(send_upstream, "ep", split_axis=0, concat_axis=0, tiled=True),
        lax.all_to_all(send_gates, "ep", split_axis=0, concat_axis=0, tiled=True),
    )
    both_tokens, both_upstream, both_gates = (
        lax.all_gather(arrived_tokens, "grp", axis=0, tiled=True),
        lax.all_gather(arrived_upstream, "grp", axis=0, tiled=True),
        lax.all_gather(arrived_gates, "grp", axis=0, tiled=True),
    )
    grad_pre_gate, grad_pre_up, grad_gate, grad_up, grad_down = expert_backward(
        both_tokens.reshape(-1, model_width),
        both_upstream.reshape(-1, model_width),
        both_gates.reshape(-1),
        gate_half,
        up_half,
        down_half,
    )
    summed = lax.psum_scatter(
        input_rows(grad_pre_gate, grad_pre_up, gate_half, up_half),
        "grp",
        scatter_dimension=0,
        tiled=True,
    )
    returned = lax.all_to_all(
        summed.astype(jnp.bfloat16).reshape(arrived_tokens.shape),
        "ep",
        split_axis=0,
        concat_axis=0,
        tiled=True,
    )
    grad_gate = grad_gate.astype(jnp.bfloat16)
    grad_up = grad_up.astype(jnp.bfloat16)
    grad_down = grad_down.astype(jnp.bfloat16)
    picked_rows = returned.reshape(-1, model_width)[expert_ids.reshape(-1) * capacity + slot_index]
    grad_input = jnp.sum(
        picked_rows.astype(jnp.float32).reshape(tok_count, top_count, model_width), axis=1
    ).astype(jnp.bfloat16)
    return (grad_input, grad_gate[None], grad_up[None], grad_down[None])


def solution(mesh):
    return jax.shard_map(
        local,
        mesh=mesh,
        in_specs=(
            P(("grp", "ep"), None),
            P(("grp", "ep"), None),
            P(("grp", "ep"), None),
            P(("grp", "ep"), None),
            P("ep", None, "grp"),
            P("ep", None, "grp"),
            P("ep", "grp", None),
        ),
        out_specs=(
            P(("grp", "ep"), None),
            P("ep", None, "grp"),
            P("ep", None, "grp"),
            P("ep", "grp", None),
        ),
        check_vma=False,
    )
```

profile of v0, /device:TPU:32, one launch (start us, length us, event | category | flops | bytes accessed | tf_op | source)
XLA Modules:
  0.0 539.0 jit_solution(1032815372370136302)
XLA Ops:
  8.9 22.0 %scatter_fusion = s32[128,5]{0,1:T(8,128)S(1)} fusion(s32[128,5]{0,1:T(8,128)S(1)} %broadcast_in_dim.51, s32[512]{0:T(512)S(1)} %bitcast.56, s32[512]{0:T(512)S(1)} %iota.23), kind=kCustom, calls=%fused_computation.4 | custom fusion | bytes 10240 | tf_op jit(solution)/shard_map/scatter | solution.py:26
  35.5 5.5 %reshape.203 = bf16[128,5,2048]{2,1,0:T(8,128)(2,1)} reshape(bf16[640,2048]{1,0:T(8,128)(2,1)} %gather_fusion.1) | data formatting | bytes 5242880 | tf_op jit(solution)/shard_map/gather | solution.py:72
  45.1 5.5 %reshape.211 = bf16[128,5,2048]{2,1,0:T(8,128)(2,1)} reshape(bf16[640,2048]{1,0:T(8,128)(2,1)} %gather_fusion.2) | data formatting | bytes 5242880 | tf_op jit(solution)/shard_map/gather | solution.py:71
  50.6 5.2 broadcast_select_fusion.1
  55.8 111.0 %all_to_all.27 = bf16[128,5,2048]{2,1,0:T(8,128)(2,1)S(1)} all-to-all(bf16[128,5,2048]{2,1,0:T(8,128)(2,1)S(1)} %get-tuple-element.9), channel_id=1, replica_groups=mesh['grp'=2,'ep'=128] {'ep'}, dimensions={0} | all-to-all | bytes 5242880 | tf_op jit(solution)/shard_map/all_to_all | solution.py:88
  170.1 104.5 %all_to_all.28 = bf16[128,5,2048]{2,1,0:T(8,128)(2,1)S(1)} all-to-all(bf16[128,5,2048]{2,1,0:T(8,128)(2,1)} %get-tuple-element.8), channel_id=1, replica_groups=mesh['grp'=2,'ep'=128] {'ep'}, dimensions={0} | all-to-all | bytes 5242880 | tf_op jit(solution)/shard_map/all_to_all | solution.py:89
  283.6 19.9 %all_to_all.29 = bf16[128,1,5]{2,1,0:T(2,128)(2,1)S(1)} all-to-all(bf16[128,1,5]{2,1,0:T(2,128)(2,1)S(1)} %copy.51), channel_id=1, replica_groups=mesh['grp'=2,'ep'=128] {'ep'}, dimensions={0} | all-to-all | bytes 2560 | tf_op jit(solution)/shard_map/all_to_all | solution.py:90
  305.7 8.9 %copy.59 = bf16[256,5,2048]{2,1,0:T(8,128)(2,1)} copy(bf16[256,5,2048]{2,0,1:T(8,128)(2,1)} %all-gather.6.cloned.1.call-done) | data formatting | bytes 10485760 | tf_op jit(solution)/shard_map/all_gather | solution.py:93
  314.6 10.0 %reshape.190 = bf16[1280,2048]{1,0:T(8,128)(2,1)} reshape(bf16[256,5,2048]{2,1,0:T(8,128)(2,1)} %copy.59) | data formatting | bytes 10485760 | tf_op jit(solution)/shard_map/reshape | solution.py:98
  324.6 6.8 %fusion.6 = f32[1280,384]{1,0:T(8,128)} fusion(bf16[1280,2048]{1,0:T(8,128)(2,1)} %reshape.190, bf16[1,2048,384]{2,1,0:T(8,128)(2,1)S(1)} %copy-done), kind=kOutput, calls=%fused_computation.22 | convolution fusion | flops 2013265920 | bytes 8781824 | tf_op jit(solution)/shard_map/dot_general | solution.py:45
  331.4 4.3 fusion.9
  335.8 8.9 %copy.57 = bf16[256,5,2048]{2,1,0:T(8,128)(2,1)} copy(bf16[256,5,2048]{2,0,1:T(8,128)(2,1)} %all-gather.4.cloned.1.call-done) | data formatting | bytes 10485760 | tf_op jit(solution)/shard_map/all_gather | solution.py:94
  344.7 10.4 %reshape.189 = bf16[1280,2048]{1,0:T(8,128)(2,1)} reshape(bf16[256,5,2048]{2,1,0:T(8,128)(2,1)} %copy.57) | data formatting | bytes 10485760 | tf_op jit(solution)/shard_map/reshape | solution.py:99
  355.1 7.6 %multiply_convert_fusion.1 = (bf16[1280,384]{1,0:T(8,128)(2,1)S(1)}, bf16[1280,384]{1,0:T(8,128)(2,1)S(1)}) fusion(f32[1280,384]{1,0:T(8,128)} %fusion.6, f32[1280,384]{1,0:T(8,128)} %fusion.9, bf16[1280,2048]{1,0:T(8,128)(2,1)} %reshape.189, bf16[1,384,2048]{2,1,0:T(8,128)(2,1)} %param.13, f32[1280]{0:T(1024)S(1)} %reshape.193), kind=kOutput, calls=%fused_computation.16 | convolution fusion | flops 2020147200 | bytes 12719104 | tf_op jit(solution)/shard_map/dot_general | solution.py:39
  365.6 5.7 %convolution_add_fusion = f32[1280,2048]{1,0:T(8,128)} fusion(f32[1280,2048]{1,0:T(8,128)S(1)} %fusion.4, bf16[1280,384]{1,0:T(8,128)(2,1)S(1)} %get-tuple-element.6, bf16[1,2048,384]{2,1,0:T(8,128)(2,1)S(1)} %copy-done.5), kind=kOutput, calls=%fused_computation.5 | convolution fusion | flops 2015887360 | bytes 23527424 | tf_op jit(solution)/shard_map/dot_general | solution.py:39
  371.4 18.2 %reduce-scatter.2.cloned.1.call-done = f32[640,2048]{1,0:T(8,128)} async-done(((f32[1280,2048]{1,0:T(8,128)}), f32[640,2048]{1,0:T(8,128)}) %reduce-scatter.2.cloned.1.call-update) | async-done | bytes 5242896 | tf_op jit(solution)/shard_map/reduce_scatter | solution.py:105
  389.5 4.4 convert_element_type.88
  393.9 5.5 %reshape.191 = bf16[128,5,2048]{2,1,0:T(8,128)(2,1)} reshape(bf16[640,2048]{1,0:T(8,128)(2,1)} %convert_element_type.88) | data formatting | bytes 5242880 | tf_op jit(solution)/shard_map/reshape | solution.py:112
  399.4 14.6 %all-to-all-start.3 = ((bf16[128,5,2048]{2,1,0:T(8,128)(2,1)}), bf16[128,5,2048]{2,1,0:T(8,128)(2,1)}, u32[]{:S(2)}, u32[]{:S(2)}) async-start(bf16[128,5,2048]{2,1,0:T(8,128)(2,1)} %reshape.191), calls=%async_computation.4 | async-start | bytes 8388608 | tf_op jit(solution)/shard_map/all_to_all | solution.py:111
  414.1 7.0 %fusion.1 = bf16[1,2048,384]{2,1,0:T(8,128)(2,1)} fusion(bf16[1280,2048]{1,0:T(8,128)(2,1)} %reshape.190, bf16[1280,384]{1,0:T(8,128)(2,1)} %copy-done.4), kind=kOutput, calls=%fused_computation.13 | convolution fusion | flops 2014052352 | bytes 7798784 | tf_op jit(solution)/shard_map/dot_general | solution.py:33
  428.9 81.4 %all-to-all-done.3 = bf16[128,5,2048]{2,1,0:T(8,128)(2,1)} async-done(((bf16[128,5,2048]{2,1,0:T(8,128)(2,1)}), bf16[128,5,2048]{2,1,0:T(8,128)(2,1)}, u32[]{:S(2)}, u32[]{:S(2)}) %all-to-all-start.3) | async-done | bytes 2621472 | tf_op jit(solution)/shard_map/all_to_all | solution.py:111
  510.3 5.6 %reshape.192 = bf16[640,2048]{1,0:T(8,128)(2,1)} reshape(bf16[128,5,2048]{2,1,0:T(8,128)(2,1)} %all-to-all-done.3) | data formatting | bytes 5242880 | tf_op jit(solution)/shard_map/reshape | solution.py:121
  516.0 7.3 %gather_fusion.3 = bf16[512,2048]{1,0:T(8,128)(2,1)} fusion(bf16[640,2048]{1,0:T(8,128)(2,1)} %reshape.192, s32[1024]{0:T(1024)S(1)} %pad_clamp_fusion), kind=kCustom, calls=%fused_computation.3 | custom fusion | bytes 4196352 | tf_op jit(solution)/shard_map/gather | solution.py:121
  527.4 5.0 reduce_sum.32
  (79 shorter events, 39.6 us)
Async XLA Ops:
  7.2 317.5 %copy-start = (bf16[1,2048,384]{2,1,0:T(8,128)(2,1)S(1)}, bf16[1,2048,384]{2,1,0:T(8,128)(2,1)}, u32[]{:S(2)}) copy-start(bf16[1,2048,384]{2,1,0:T(8,128)(2,1)} %param.11) | copy-start | bytes 4718596
  7.2 298.5 %all-gather.6.cloned.1.call-start = ((), (), s32[]{:S(2)}) async-start(), calls=%async_computation.6 | async-start | bytes 7864320 | tf_op jit(solution)/shard_map/all_gather | solution.py:93
  8.9 22.5 %copy-start.1 = (bf16[128,2048]{1,0:T(8,128)(2,1)S(1)}, bf16[128,2048]{1,0:T(8,128)(2,1)}, u32[]{:S(2)}) copy-start(bf16[128,2048]{1,0:T(8,128)(2,1)} %param.8) | copy-start | bytes 1572868
  35.5 5.5 %copy-start.2 = (bf16[128,2048]{1,0:T(8,128)(2,1)S(1)}, bf16[128,2048]{1,0:T(8,128)(2,1)}, u32[]{:S(2)}) copy-start(bf16[128,2048]{1,0:T(8,128)(2,1)} %param.7) | copy-start | bytes 1572868
  170.1 165.7 %all-gather.4.cloned.1.call-start = ((), (), s32[]{:S(2)}) async-start(), calls=%async_computation.5 | async-start | bytes 7864320 | tf_op jit(solution)/shard_map/all_gather | solution.py:94
  277.9 0.7 copy-start.8
  277.9 111.6 %reduce-scatter.2.cloned.1.call-start = ((), (), s32[]{:S(2)}) async-start(), calls=%async_computation.7 | async-start | bytes 15728640 | tf_op jit(solution)/shard_map/reduce_scatter | solution.py:105
  324.6 6.8 %copy-start.3 = (bf16[1280,2048]{1,0:T(8,128)(2,1)S(1)}, bf16[1280,2048]{1,0:T(8,128)(2,1)}, u32[]{:S(2)}) copy-start(bf16[1280,2048]{1,0:T(8,128)(2,1)} %reshape.190) | copy-start | bytes 15728644
  324.6 6.8 %copy-start.5 = (bf16[1,2048,384]{2,1,0:T(8,128)(2,1)S(1)}, bf16[1,2048,384]{2,1,0:T(8,128)(2,1)}, u32[]{:S(2)}) copy-start(bf16[1,2048,384]{2,1,0:T(8,128)(2,1)} %param.12) | copy-start | bytes 4718596
  362.7 3.0 copy-start.6
  362.7 3.0 copy-start.4
  399.4 21.7 %slice-start = ((s8[5242880]{0:T(1024)(128)(4,1)}), s8[1048576]{0:T(1024)(128)(4,1)S(1)}, s32[]{:S(2)}) async-start(s8[5242880]{0:T(1024)(128)(4,1)} %bitcast.57), calls=%async_computation.8 | async-start | bytes 2097152
  399.4 110.9 %all-to-all-start.3 = ((bf16[128,5,2048]{2,1,0:T(8,128)(2,1)}), bf16[128,5,2048]{2,1,0:T(8,128)(2,1)}, u32[]{:S(2)}, u32[]{:S(2)}) async-start(bf16[128,5,2048]{2,1,0:T(8,128)(2,1)} %reshape.191), calls=%async_computation.4 | async-start | bytes 8388608 | tf_op jit(solution)/shard_map/all_to_all | solution.py:111
  414.1 7.0 %slice-start.1 = ((s8[5242880]{0:T(1024)(128)(4,1)}), s8[4194304]{0:T(1024)(128)(4,1)S(1)}, s32[]{:S(2)}) async-start(s8[5242880]{0:T(1024)(128)(4,1)} %bitcast.57), calls=%async_computation.9 | async-start | bytes 8388608
  414.1 7.0 %copy-start.7 = (bf16[1280,384]{1,0:T(8,128)(2,1)S(1)}, bf16[1280,384]{1,0:T(8,128)(2,1)}, u32[]{:S(2)}) copy-start(bf16[1280,384]{1,0:T(8,128)(2,1)} %copy-done.6) | copy-start | bytes 2949124
  414.1 11.1 %slice-start.2 = ((s8[5242880]{0:T(1024)(128)(4,1)}), s8[4194304]{0:T(1024)(128)(4,1)S(1)}, s32[]{:S(2)}) async-start(s8[5242880]{0:T(1024)(128)(4,1)} %bitcast.59), calls=%async_computation.10 | async-start | bytes 8388608
  421.1 4.1 slice-start.3
  421.1 4.1 copy-start.9
  421.1 4.1 copy-start.10
Sparse Core Ops, SparseCore 0:
  170.2 16.6 all-gather.5
  278.0 16.8 all-gather.3
  371.5 17.9 reduce-scatter.1
where the time goes:
time: 548 us; the launch traced here: 539 us
  blocking collectives  237 us (43%)
  local copies, waits for them, and re-layouts  116 us (21%)
  waiting for transfers between devices  99.7 us (18%)
  matrix products  42.3 us (8%)
  starting transfers between devices  14.8 us (3%)
  other arithmetic  14.8 us (3%)
  between operations  14.3 us (3%)
    all_to_all x1, blocking collectives, local(): lax.all_to_all(send_tokens, 'ep', split_axis=0, concat_axis=0, tiled=True)  111 us
    all_to_all x1, blocking collectives, local(): lax.all_to_all(send_upstream, 'ep', split_axis=0, concat_axis=0, tiled=True)  105 us
    all_to_all x1, waiting for transfers between devices, local(): lax.all_to_all(summed.astype(jnp.bfloat16).reshape(arrived_tokens.shape),...  81.4 us
    scatter x1, local copies, waits for them, and re-layouts, routing_table(): source_table.at[flattened, slot_index]  22 us
    all_to_all x1, blocking collectives, local(): lax.all_to_all(send_gates, 'ep', split_axis=0, concat_axis=0, tiled=True)  19.9 us
    reduce_scatter x1, waiting for transfers between devices, local(): lax.psum_scatter(input_rows(grad_pre_gate, grad_pre_up, gate_half, up_hal...  18.2 us
    dot_general x3, matrix products, contract_last(): lax.dot_general(left, right, (((1,), (1,)), ((), ())), preferred_element_...  16.2 us
    dot_general x3, matrix products, contract_rows(): lax.dot_general(left, right, (((0,), (0,)), ((), ())), preferred_element_...  14.7 us
  transfers between devices with their start and end apart: 4, of which 2 were waited for; matrix products, arithmetic and copies ran while one was open for 10% of the time, Pallas kernels for 0%

commit v1 on v0

v1 whole, which is shorter than its diff:
```python
import jax
import jax.numpy as jnp
from jax import lax
from jax.experimental import pallas as pl
from jax.experimental.pallas import tpu as pltpu
from jax.sharding import PartitionSpec as P

CAP = 5
VMEM = pl.BlockSpec(memory_space=pltpu.VMEM)
SMEM = pl.BlockSpec(memory_space=pltpu.SMEM)


def slot_kernel(ids, gates, x, dy, send_x, send_dy, place, count):
    tokens, experts = x.shape[0], count.shape[0]

    def clear_count(e, carry):
        count[e] = 0
        return carry

    lax.fori_loop(0, experts, clear_count, 0, unroll=8)
    send_x[...] = jnp.zeros_like(send_x)
    send_dy[...] = jnp.zeros_like(send_dy)

    def one_token(t, carry):
        x_row = x[t]
        dy_row = dy[t].astype(jnp.float32)
        for k in range(4):
            pair = t * 4 + k
            expert = ids[pair]
            taken = count[expert]
            count[expert] = taken + 1
            slot = expert * CAP + taken
            place[pair] = slot
            send_x[slot] = x_row
            send_dy[slot] = (dy_row * gates[pair]).astype(jnp.bfloat16)
        return carry

    lax.fori_loop(0, tokens, one_token, 0, unroll=2)


def fill_slots(ids, gates, x, dy, experts):
    rows = experts * CAP
    out = jax.ShapeDtypeStruct((rows,) + x.shape[1:], jnp.bfloat16)
    return pl.pallas_call(
        slot_kernel,
        out_shape=(out, out, jax.ShapeDtypeStruct(ids.shape, jnp.int32)),
        in_specs=[SMEM, SMEM, VMEM, VMEM],
        out_specs=(VMEM, VMEM, SMEM),
        scratch_shapes=[pltpu.SMEM((experts,), jnp.int32)],
        compiler_params=pltpu.CompilerParams(vmem_limit_bytes=32 * 2**20),
        name="fill_slots",
    )(ids, gates, x, dy)


def combine_kernel(place, rows, out):
    def one_token(t, carry):
        total = rows[place[4 * t]].astype(jnp.float32)
        for k in range(1, 4):
            total = total + rows[place[4 * t + k]].astype(jnp.float32)
        out[t] = total.astype(jnp.bfloat16)
        return carry

    lax.fori_loop(0, out.shape[0], one_token, 0, unroll=2)


def combine(place, rows, tokens):
    return pl.pallas_call(
        combine_kernel,
        out_shape=jax.ShapeDtypeStruct((tokens,) + rows.shape[1:], jnp.bfloat16),
        in_specs=[SMEM, VMEM],
        out_specs=VMEM,
        compiler_params=pltpu.CompilerParams(vmem_limit_bytes=32 * 2**20),
        name="combine",
    )(place, rows)


def contract(left, right, dims):
    return lax.dot_general(left, right, (dims, ((), ())), preferred_element_type=jnp.float32)


def local(activations, out_grad, expert_ids, gate_values, w_gate, w_up, w_down):
    experts = lax.axis_size("ep")
    tokens, width = activations.shape
    lanes = (width // 128, 128)
    swap = lambda a: lax.ppermute(a, "grp", [(0, 1), (1, 0)])
    exchange = lambda a: lax.all_to_all(a, "ep", split_axis=0, concat_axis=0, tiled=True)

    send_x, send_dy, place = fill_slots(
        expert_ids.reshape(-1),
        gate_values.reshape(-1).astype(jnp.float32),
        activations.reshape((tokens,) + lanes),
        out_grad.reshape((tokens,) + lanes),
        experts,
    )
    gate_w = jnp.concatenate([w_gate[0], swap(w_gate[0])], axis=1)
    up_w = jnp.concatenate([w_up[0], swap(w_up[0])], axis=1)
    down_w = jnp.concatenate([w_down[0], swap(w_down[0])], axis=0)

    x = exchange(send_x).reshape(-1, width)
    pre_gate = contract(x, gate_w, ((1,), (0,)))
    pre_up = contract(x, up_w, ((1,), (0,)))
    sig = jax.nn.sigmoid(pre_gate)
    silu = pre_gate * sig
    weighted = (silu * pre_up).astype(jnp.bfloat16)

    dy = exchange(send_dy).reshape(-1, width)
    grad_hidden = contract(dy, down_w, ((1,), (1,)))
    grad_pre_gate = (grad_hidden * pre_up * sig * (1.0 + pre_gate * (1.0 - sig))).astype(jnp.bfloat16)
    grad_pre_up = (grad_hidden * silu).astype(jnp.bfloat16)
    row_grad = (
        contract(grad_pre_gate, gate_w, ((1,), (1,))) + contract(grad_pre_up, up_w, ((1,), (1,)))
    ).astype(jnp.bfloat16)
    returned = exchange(row_grad.reshape((-1,) + lanes))

    half = w_gate.shape[2]
    rows_t = ((0,), (0,))
    theirs = swap(
        (
            contract(x, grad_pre_gate[:, half:], rows_t).astype(jnp.bfloat16),
            contract(x, grad_pre_up[:, half:], rows_t).astype(jnp.bfloat16),
            contract(weighted[:, half:], dy, rows_t).astype(jnp.bfloat16),
        )
    )
    mine = (
        contract(x, grad_pre_gate[:, :half], rows_t),
        contract(x, grad_pre_up[:, :half], rows_t),
        contract(weighted[:, :half], dy, rows_t),
    )
    grads = [(m + t.astype(jnp.float32)).astype(jnp.bfloat16)[None] for m, t in zip(mine, theirs)]
    grad_input = combine(place, returned, tokens).reshape(tokens, width)
    return (grad_input, *grads)


def solution(mesh):
    tokens = P(("grp", "ep"), None)
    columns, rows = P("ep", None, "grp"), P("ep", "grp", None)
    return jax.shard_map(
        local,
        mesh=mesh,
        in_specs=(tokens, tokens, tokens, tokens, columns, columns, rows),
        out_specs=(tokens, columns, columns, rows),
        check_vma=False,
    )
```

time: 548 us -> 252 us (0.46); the launches traced: 539 us -> 251 us
  blocking collectives: 237 us -> 79.2 us
  local copies, waits for them, and re-layouts: 116 us -> 7.38 us
  other arithmetic: 14.8 us -> 0 us
  between operations: 14.3 us -> 0.87 us
  Pallas kernels: 0 us -> 7.12 us
    all_to_all x3 -> x1, blocking collectives: 235 us -> 79.2 us  [local(): lax.all_to_all(a, 'ep', split_axis=0, concat_axis=0, tiled=True)]
    gather x9 -> x0, local copies, waits for them, and re-layouts: 35.2 us -> none  [the longest x2 11.4 us: local(): returned.reshape(-1, model_width)]
    reshape x6 -> x1, local copies, waits for them, and re-layouts: 31.7 us -> 0.1 us  [local(): expert_ids.reshape(-1)]
    scatter x1 -> x0, local copies, waits for them, and re-layouts: 22 us -> none  [routing_table(): source_table.at[flattened, slot_index]]
    reduce_scatter x1 -> x0, waiting for transfers between devices: 18.2 us -> none  [local(): lax.psum_scatter(input_rows(grad_pre_gate, grad_pre_up, gate_half, up_hal...]
    all_gather x2 -> x0, local copies, waits for them, and re-layouts: 17.8 us -> none  [the longest x1 8.91 us: local(): lax.all_gather(arrived_tokens, 'grp', axis=0, tiled=True)]
    all_to_all x1 -> x2, waiting for transfers between devices: 81.4 us -> 97 us  [local(): lax.all_to_all(a, 'ep', split_axis=0, concat_axis=0, tiled=True)]
    pallas_call x0 -> x2, Pallas kernels: none -> 7.12 us  [the longest x1 5.55 us: fill_slots(): pl.pallas_call(slot_kernel, out_shape=(out, out, jax.ShapeDtypeStruct(ids...]
  transfers between devices with their start and end apart: 4 -> 8, of which waited for: 2 -> 3; matrix products, arithmetic and copies ran while one was open for 10% -> 11% of each run, Pallas kernels for 0% -> 0%
where the time goes in v1:
time: 252 us; the launch traced here: 251 us
  waiting for transfers between devices  101 us (40%)
  blocking collectives  79.2 us (31%)
  matrix products  39.8 us (16%)
  starting transfers between devices  15.4 us (6%)
  local copies, waits for them, and re-layouts  7.38 us (3%)
  Pallas kernels  7.12 us (3%)
    all_to_all x2, waiting for transfers between devices, local(): lax.all_to_all(a, 'ep', split_axis=0, concat_axis=0, tiled=True)  97 us
    all_to_all x1, blocking collectives, local(): lax.all_to_all(a, 'ep', split_axis=0, concat_axis=0, tiled=True)  79.2 us
    dot_general x11, matrix products, contract(): lax.dot_general(left, right, (dims, ((), ())), preferred_element_type=jnp...  39.8 us
    all_to_all x2, starting transfers between devices, local(): lax.all_to_all(a, 'ep', split_axis=0, concat_axis=0, tiled=True)  14 us
    unnamed x29, local copies, waits for them, and re-layouts  6.37 us
    pallas_call x1, Pallas kernels, fill_slots(): pl.pallas_call(slot_kernel, out_shape=(out, out, jax.ShapeDtypeStruct(ids...  5.55 us
  transfers between devices with their start and end apart: 8, of which 3 were waited for; matrix products, arithmetic and copies ran while one was open for 11% of the time, Pallas kernels for 0%

profile of v1, /device:TPU:32, one launch (start us, length us, event | category | flops | bytes accessed | tf_op | source)
XLA Modules:
  0.0 251.0 jit_solution(9145703135421549720)
XLA Ops:
  0.6 1.1 copy.13
  1.8 1.1 copy.14
  3.8 0.8 copy.12
  4.7 5.5 %fill_slots.1 = (bf16[640,16,128]{2,1,0:T(8,128)(2,1)S(1)}, bf16[640,16,128]{2,1,0:T(8,128)(2,1)}, s32[512]{0:T(512)S(1)}) custom-call(s32[512]{0:T(512)S(1)} %reshape.32.ids, f32[512]{0:T(512)S(1)} %reshape.39.gates, bf16[128,16,128]{2,1,0:T(8,128)(2,1)S(1)} %bitcast.58, bf16[128,16,128]{2,1,0:T(8,128)(2,1)S(1)} %bitcast.59), custom_call_target="tpu_custom_call" | custom-call | tf_op jit(solution)/shard_map/fill_slots/pallas_call | solution.py:44
  10.3 79.2 %all_to_all.15 = bf16[640,16,128]{2,1,0:T(8,128)(2,1)S(1)} all-to-all(bf16[640,16,128]{2,1,0:T(8,128)(2,1)S(1)} %get-tuple-element.9), channel_id=1, replica_groups=mesh['grp'=2,'ep'=128] {'ep'}, dimensions={0} | all-to-all | bytes 5242880 | tf_op jit(solution)/shard_map/all_to_all | solution.py:86
  89.5 7.1 %all-to-all-start = ((bf16[640,16,128]{2,1,0:T(8,128)(2,1)}), bf16[640,16,128]{2,1,0:T(8,128)(2,1)}, u32[]{:S(2)}, u32[]{:S(2)}) async-start(bf16[640,16,128]{2,1,0:T(8,128)(2,1)} %get-tuple-element.8), calls=%async_computation | async-start | bytes 5242880 | tf_op jit(solution)/shard_map/all_to_all | solution.py:86
  97.3 4.2 %collective-permute-done.2 = bf16[2048,384]{1,0:T(8,128)(2,1)S(1)} collective-permute-done((bf16[2048,384]{1,0:T(8,128)(2,1)}, bf16[2048,384]{1,0:T(8,128)(2,1)S(1)}, u32[]{:S(2)}, u32[]{:S(2)}) %collective-permute-start.2) | collective-permute-done | bytes 1572896 | tf_op jit(solution)/shard_map/ppermute | solution.py:85
  101.5 5.5 %fusion.10 = f32[640,768]{1,0:T(8,128)} fusion(bf16[2048,384]{1,0:T(8,128)(2,1)S(1)} %collective-permute-done.2, bf16[2048,384]{1,0:T(8,128)(2,1)} %bitcast.77, bf16[80,8,16,128]{3,2,1,0:T(8,128)(2,1)S(1)} %bitcast.62), kind=kOutput, calls=%fused_computation.19 | convolution fusion | flops 2019557376 | bytes 7733248 | tf_op jit(solution)/shard_map/dot_general | solution.py:78
  107.1 52.7 %all-to-all-done = bf16[640,16,128]{2,1,0:T(8,128)(2,1)} async-done(((bf16[640,16,128]{2,1,0:T(8,128)(2,1)}), bf16[640,16,128]{2,1,0:T(8,128)(2,1)}, u32[]{:S(2)}, u32[]{:S(2)}) %all-to-all-start) | async-done | bytes 2621472 | tf_op jit(solution)/shard_map/all_to_all | solution.py:86
  159.8 5.1 %fusion = f32[640,768]{1,0:T(8,128)S(1)} fusion(bf16[384,2048]{1,0:T(8,128)(2,1)} %collective-permute-done, bf16[384,2048]{1,0:T(8,128)(2,1)} %bitcast.72, bf16[80,8,16,128]{3,2,1,0:T(8,128)(2,1)} %bitcast.10), kind=kOutput, calls=%fused_computation.1 | convolution fusion | flops 2019557376 | bytes 7733248 | tf_op jit(solution)/shard_map/dot_general | solution.py:78
  164.9 5.1 %multiply_convert_fusion = (bf16[640,768]{1,0:T(8,128)(2,1)}, bf16[640,768]{1,0:T(8,128)(2,1)S(1)}, bf16[640,768]{1,0:T(8,128)(2,1)S(1)}) fusion(f32[640,768]{1,0:T(8,128)S(1)} %copy-done.11, f32[640,768]{1,0:T(8,128)S(1)} %fusion, bf16[2048,384]{1,0:T(8,128)(2,1)} %collective-permute-done.1, bf16[2048,384]{1,0:T(8,128)(2,1)S(1)} %bitcast.74, ...), kind=kOutput, calls=%fused_computation.34 | convolution fusion | flops 2026930176 | bytes 12648448 | tf_op jit(solution)/shard_map/dot_general | solution.py:78
  170.1 4.4 %fusion.33 = f32[640,2048]{1,0:T(8,128)S(1)} fusion(bf16[640,768]{1,0:T(8,128)(2,1)S(1)} %get-tuple-element.12, bf16[2048,384]{1,0:T(8,128)(2,1)} %collective-permute-done.1, bf16[2048,384]{1,0:T(8,128)(2,1)S(1)} %bitcast.75), kind=kOutput, calls=%fused_computation.30 | convolution fusion | flops 2019557376 | bytes 9371648 | tf_op jit(solution)/shard_map/dot_general | solution.py:78
  174.5 2.2 fusion.38
  176.7 2.3 copy.17
  179.0 6.9 %all-to-all-start.2 = ((bf16[640,16,128]{2,1,0:T(8,128)(2,1)}), bf16[640,16,128]{2,1,0:T(8,128)(2,1)S(1)}, u32[]{:S(2)}, u32[]{:S(2)}) async-start(bf16[640,16,128]{2,1,0:T(8,128)(2,1)} %bitcast.61), calls=%async_computation.2 | async-start | bytes 5242880 | tf_op jit(solution)/shard_map/all_to_all | solution.py:86
  185.9 3.5 %convolution_convert_fusion = bf16[384,2048]{1,0:T(8,128)(2,1)S(1)} fusion(bf16[80,8,16,128]{3,2,1,0:T(8,128)(2,1)} %bitcast.10, bf16[640,768]{1,0:T(8,128)(2,1)} %get-tuple-element.10), kind=kOutput, calls=%fused_computation.10 | convolution fusion | flops 1007419392 | bytes 4685824 | tf_op jit(solution)/shard_map/dot_general | solution.py:78
  189.5 1.8 convolution_convert_fusion.1
  191.9 1.8 convolution_convert_fusion.2
  193.8 4.4 %fusion.30 = bf16[1,384,2048]{2,1,0:T(8,128)(2,1)} fusion(bf16[384,2048]{1,0:T(8,128)(2,1)S(1)} %collective-permute-done.5, bf16[80,8,16,128]{3,2,1,0:T(8,128)(2,1)} %bitcast.10, bf16[640,768]{1,0:T(8,128)(2,1)S(1)} %copy-done.6), kind=kOutput, calls=%fused_computation.29 | convolution fusion | flops 1008992256 | bytes 6258688 | tf_op jit(solution)/shard_map/dot_general | solution.py:78
  198.2 3.0 %fusion.27 = bf16[1,2048,384]{2,1,0:T(8,128)(2,1)} fusion(bf16[2048,384]{1,0:T(8,128)(2,1)S(1)} %collective-permute-done.4, bf16[80,8,16,128]{3,2,1,0:T(8,128)(2,1)S(1)} %bitcast.66, bf16[640,768]{1,0:T(8,128)(2,1)S(1)} %copy-done.8), kind=kOutput, calls=%fused_computation.28 | convolution fusion | flops 1008992256 | bytes 6258688 | tf_op jit(solution)/shard_map/dot_general | solution.py:78
  201.2 3.0 %fusion.24 = bf16[1,2048,384]{2,1,0:T(8,128)(2,1)} fusion(bf16[2048,384]{1,0:T(8,128)(2,1)S(1)} %collective-permute-done.3, bf16[80,8,16,128]{3,2,1,0:T(8,128)(2,1)S(1)} %bitcast.67, bf16[640,768]{1,0:T(8,128)(2,1)S(1)} %copy-done.10), kind=kOutput, calls=%fused_computation.27 | convolution fusion | flops 1008992256 | bytes 6258688 | tf_op jit(solution)/shard_map/dot_general | solution.py:78
  204.2 44.3 %all-to-all-done.2.rows = bf16[640,16,128]{2,1,0:T(8,128)(2,1)S(1)} async-done(((bf16[640,16,128]{2,1,0:T(8,128)(2,1)}), bf16[640,16,128]{2,1,0:T(8,128)(2,1)S(1)}, u32[]{:S(2)}, u32[]{:S(2)}) %all-to-all-start.2) | async-done | bytes 2621472 | tf_op jit(solution)/shard_map/all_to_all | solution.py:86
  248.5 1.6 combine.1
  250.1 0.9 copy.58
  (38 shorter events, 2.5 us)
Async XLA Ops:
  89.5 75.4 %copy-start = (bf16[640,16,128]{2,1,0:T(8,128)(2,1)}, bf16[640,16,128]{2,1,0:T(8,128)(2,1)S(1)}, u32[]{:S(2)}) copy-start(bf16[640,16,128]{2,1,0:T(8,128)(2,1)S(1)} %all_to_all.15) | copy-start | bytes 7864324
  89.5 70.3 %all-to-all-start = ((bf16[640,16,128]{2,1,0:T(8,128)(2,1)}), bf16[640,16,128]{2,1,0:T(8,128)(2,1)}, u32[]{:S(2)}, u32[]{:S(2)}) async-start(bf16[640,16,128]{2,1,0:T(8,128)(2,1)} %get-tuple-element.8), calls=%async_computation | async-start | bytes 5242880 | tf_op jit(solution)/shard_map/all_to_all | solution.py:86
  96.6 4.9 %collective-permute-start.2 = (bf16[2048,384]{1,0:T(8,128)(2,1)}, bf16[2048,384]{1,0:T(8,128)(2,1)S(1)}, u32[]{:S(2)}, u32[]{:S(2)}) collective-permute-start(bf16[2048,384]{1,0:T(8,128)(2,1)} %bitcast.76), channel_id=1, source_target_pairs={{0,128},{128,0},{1,129},{129,1},{2,130},{130,2},{3,131},{131,3},{4... | collective-permute-start | bytes 4718600 | tf_op jit(solution)/shard_map/ppermute | solution.py:85
  96.7 10.4 %collective-permute-start = (bf16[384,2048]{1,0:T(8,128)(2,1)}, bf16[384,2048]{1,0:T(8,128)(2,1)}, u32[]{:S(2)}, u32[]{:S(2)}) collective-permute-start(bf16[384,2048]{1,0:T(8,128)(2,1)} %bitcast.71), channel_id=1, source_target_pairs={{0,128},{128,0},{1,129},{129,1},{2,130},{130,2},{3,131},{131,3},{4... | collective-permute-start | bytes 4718600 | tf_op jit(solution)/shard_map/ppermute | solution.py:85
  97.2 67.7 %collective-permute-start.1 = (bf16[2048,384]{1,0:T(8,128)(2,1)}, bf16[2048,384]{1,0:T(8,128)(2,1)}, u32[]{:S(2)}, u32[]{:S(2)}) collective-permute-start(bf16[2048,384]{1,0:T(8,128)(2,1)} %bitcast.73), channel_id=1, source_target_pairs={{0,128},{128,0},{1,129},{129,1},{2,130},{130,2},{3,131},{131,3},{4... | collective-permute-start | bytes 4718600 | tf_op jit(solution)/shard_map/ppermute | solution.py:85
  101.5 5.5 %copy-start.4 = (bf16[2048,384]{1,0:T(8,128)(2,1)}, bf16[2048,384]{1,0:T(8,128)(2,1)S(1)}, u32[]{:S(2)}) copy-start(bf16[2048,384]{1,0:T(8,128)(2,1)S(1)} %collective-permute-done.2) | copy-start | bytes 4718596
  159.8 5.1 %copy-start.2 = (bf16[1,2048,384]{2,1,0:T(8,128)(2,1)S(1)}, bf16[1,2048,384]{2,1,0:T(8,128)(2,1)}, u32[]{:S(2)}) copy-start(bf16[1,2048,384]{2,1,0:T(8,128)(2,1)} %param.12) | copy-start | bytes 4718596
  159.8 5.1 %copy-start.11 = (f32[640,768]{1,0:T(8,128)S(1)}, f32[640,768]{1,0:T(8,128)}, u32[]{:S(2)}) copy-start(f32[640,768]{1,0:T(8,128)} %fusion.10) | copy-start | bytes 5898244
  170.0 4.4 %copy-start.7 = (bf16[640,768]{1,0:T(8,128)(2,1)}, bf16[640,768]{1,0:T(8,128)(2,1)S(1)}, u32[]{:S(2)}) copy-start(bf16[640,768]{1,0:T(8,128)(2,1)S(1)} %get-tuple-element.12) | copy-start | bytes 2949124
  170.0 4.4 %copy-start.9 = (bf16[640,768]{1,0:T(8,128)(2,1)}, bf16[640,768]{1,0:T(8,128)(2,1)S(1)}, u32[]{:S(2)}) copy-start(bf16[640,768]{1,0:T(8,128)(2,1)S(1)} %get-tuple-element.11) | copy-start | bytes 2949124
  170.0 4.4 %copy-start.3 = (bf16[1,2048,384]{2,1,0:T(8,128)(2,1)S(1)}, bf16[1,2048,384]{2,1,0:T(8,128)(2,1)}, u32[]{:S(2)}) copy-start(bf16[1,2048,384]{2,1,0:T(8,128)(2,1)} %param.11) | copy-start | bytes 4718596
  170.0 4.4 %copy-start.5 = (bf16[2048,384]{1,0:T(8,128)(2,1)S(1)}, bf16[2048,384]{1,0:T(8,128)(2,1)}, u32[]{:S(2)}) copy-start(bf16[2048,384]{1,0:T(8,128)(2,1)} %copy-done.4) | copy-start | bytes 4718596
  179.0 69.4 %all-to-all-start.2 = ((bf16[640,16,128]{2,1,0:T(8,128)(2,1)}), bf16[640,16,128]{2,1,0:T(8,128)(2,1)S(1)}, u32[]{:S(2)}, u32[]{:S(2)}) async-start(bf16[640,16,128]{2,1,0:T(8,128)(2,1)} %bitcast.61), calls=%async_computation.2 | async-start | bytes 5242880 | tf_op jit(solution)/shard_map/all_to_all | solution.py:86
  185.9 3.6 %copy-start.1 = (bf16[640,16,128]{2,1,0:T(8,128)(2,1)S(1)}, bf16[640,16,128]{2,1,0:T(8,128)(2,1)}, u32[]{:S(2)}) copy-start(bf16[640,16,128]{2,1,0:T(8,128)(2,1)} %copy-done) | copy-start | bytes 7864324
  185.9 3.6 %copy-start.8 = (bf16[640,768]{1,0:T(8,128)(2,1)S(1)}, bf16[640,768]{1,0:T(8,128)(2,1)}, u32[]{:S(2)}) copy-start(bf16[640,768]{1,0:T(8,128)(2,1)} %copy-done.7) | copy-start | bytes 2949124
  189.4 2.5 copy-start.10
  189.4 4.4 %collective-permute-start.5 = (bf16[384,2048]{1,0:T(8,128)(2,1)S(1)}, bf16[384,2048]{1,0:T(8,128)(2,1)S(1)}, u32[]{:S(2)}, u32[]{:S(2)}) collective-permute-start(bf16[384,2048]{1,0:T(8,128)(2,1)S(1)} %convolution_convert_fusion), channel_id=1, source_target_pairs={{0,128},{128,0},{1,129},{129,1},{2,130},{130,2},{3,131},{131,3},{4... | collective-permute-start | bytes 4718600 | tf_op jit(solution)/shard_map/ppermute | solution.py:85
  191.3 2.5 copy-start.6
  191.3 6.9 %collective-permute-start.4 = (bf16[2048,384]{1,0:T(8,128)(2,1)S(1)}, bf16[2048,384]{1,0:T(8,128)(2,1)S(1)}, u32[]{:S(2)}, u32[]{:S(2)}) collective-permute-start(bf16[2048,384]{1,0:T(8,128)(2,1)S(1)} %convolution_convert_fusion.1), channel_id=1, source_target_pairs={{0,128},{128,0},{1,129},{129,1},{2,130},{130,2},{3,131},{131,3},{4... | collective-permute-start | bytes 4718600 | tf_op jit(solution)/shard_map/ppermute | solution.py:85
  193.7 7.5 %collective-permute-start.3 = (bf16[2048,384]{1,0:T(8,128)(2,1)S(1)}, bf16[2048,384]{1,0:T(8,128)(2,1)S(1)}, u32[]{:S(2)}, u32[]{:S(2)}) collective-permute-start(bf16[2048,384]{1,0:T(8,128)(2,1)S(1)} %convolution_convert_fusion.2), channel_id=1, source_target_pairs={{0,128},{128,0},{1,129},{129,1},{2,130},{130,2},{3,131},{131,3},{4... | collective-permute-start | bytes 4718600 | tf_op jit(solution)/shard_map/ppermute | solution.py:85

commit v2 on v1

v2 whole, which is shorter than its diff:
```python
import functools

import jax
import jax.numpy as jnp
from jax import lax
from jax.experimental import pallas as pl
from jax.experimental.pallas import tpu as pltpu
from jax.sharding import PartitionSpec as P

CAP = 5
VMEM = pl.BlockSpec(memory_space=pltpu.VMEM)
SMEM = pl.BlockSpec(memory_space=pltpu.SMEM)


def fill_x_kernel(ids, x, send_x, place, count):
    top, tokens = ids.shape

    def clear_count(e, carry):
        count[e] = 0
        return carry

    lax.fori_loop(0, count.shape[0], clear_count, 0, unroll=8)
    send_x[...] = jnp.zeros_like(send_x)

    def one_token(t, carry):
        row = x[t]
        for k in range(top):
            expert = ids[k, t]
            taken = count[expert]
            count[expert] = taken + 1
            slot = expert * CAP + taken
            place[k, t] = slot
            send_x[slot] = row
        return carry

    lax.fori_loop(0, tokens, one_token, 0, unroll=2)


def fill_dy_kernel(place, gates, dy, send_dy):
    top, tokens = place.shape
    send_dy[...] = jnp.zeros_like(send_dy)

    def one_token(t, carry):
        row = dy[t].astype(jnp.float32)
        for k in range(top):
            send_dy[place[k, t]] = (row * gates[k, t]).astype(jnp.bfloat16)
        return carry

    lax.fori_loop(0, tokens, one_token, 0, unroll=2)


def fill_x(ids, x, experts):
    return pl.pallas_call(
        fill_x_kernel,
        out_shape=(
            jax.ShapeDtypeStruct((experts * CAP,) + x.shape[1:], x.dtype),
            jax.ShapeDtypeStruct(ids.shape, jnp.int32),
        ),
        in_specs=[SMEM, VMEM],
        out_specs=(VMEM, SMEM),
        scratch_shapes=[pltpu.SMEM((experts,), jnp.int32)],
        compiler_params=pltpu.CompilerParams(vmem_limit_bytes=16 * 2**20),
        name="fill_x",
    )(ids, x)


def fill_dy(place, gates, dy, experts):
    return pl.pallas_call(
        fill_dy_kernel,
        out_shape=jax.ShapeDtypeStruct((experts * CAP,) + dy.shape[1:], dy.dtype),
        in_specs=[SMEM, SMEM, VMEM],
        out_specs=VMEM,
        compiler_params=pltpu.CompilerParams(vmem_limit_bytes=16 * 2**20),
        cost_estimate=pl.CostEstimate(flops=10**7, bytes_accessed=8 * 2**20, transcendentals=0),
        name="fill_dy",
    )(place, gates, dy)


def row_grads_kernel(parts, columns, dy, slope, silu, w_down, w_gate, w_up, out, grad_gate, grad_up):
    rows, blocks, lanes = dy.shape
    width = blocks * lanes
    step, group = rows // parts, blocks // columns
    for i in range(parts):
        r = pl.ds(i * step, step)
        grad_hidden = contract(dy[r].reshape(step, width), w_down[...], ((1,), (1,)))
        grad_gate[r, :] = (grad_hidden * slope[r, :]).astype(jnp.bfloat16)
        grad_up[r, :] = (grad_hidden * silu[r, :]).astype(jnp.bfloat16)
        for c in range(columns):
            w = pl.ds(c * group * lanes, group * lanes)
            total = contract(grad_gate[r, :], w_gate[w, :], ((1,), (1,)))
            total = total + contract(grad_up[r, :], w_up[w, :], ((1,), (1,)))
            out[r, pl.ds(c * group, group), :] = total.astype(jnp.bfloat16).reshape(step, group, lanes)


def row_grads(dy, slope, silu, w_down, w_gate, w_up):
    rows, hidden = slope.shape
    part = jax.ShapeDtypeStruct((rows, hidden), jnp.bfloat16)
    return pl.pallas_call(
        functools.partial(row_grads_kernel, 2, 4),
        out_shape=(jax.ShapeDtypeStruct(dy.shape, jnp.bfloat16), part, part),
        in_specs=[VMEM] * 6,
        out_specs=(VMEM,) * 3,
        compiler_params=pltpu.CompilerParams(vmem_limit_bytes=28 * 2**20),
        cost_estimate=pl.CostEstimate(
            flops=6 * rows * w_gate.size, bytes_accessed=8 * 2**20, transcendentals=0
        ),
        name="row_grads",
    )(dy, slope, silu, w_down, w_gate, w_up)


def combine_kernel(place, rows, out):
    def one_token(t, carry):
        total = rows[place[0, t]].astype(jnp.float32)
        for k in range(1, place.shape[0]):
            total = total + rows[place[k, t]].astype(jnp.float32)
        out[t] = total.astype(jnp.bfloat16)
        return carry

    lax.fori_loop(0, out.shape[0], one_token, 0, unroll=2)


def combine(place, rows, tokens):
    return pl.pallas_call(
        combine_kernel,
        out_shape=jax.ShapeDtypeStruct((tokens,) + rows.shape[1:], jnp.bfloat16),
        in_specs=[SMEM, VMEM],
        out_specs=VMEM,
        compiler_params=pltpu.CompilerParams(vmem_limit_bytes=16 * 2**20),
        name="combine",
    )(place, rows)


def contract(left, right, dims):
    return lax.dot_general(left, right, (dims, ((), ())), preferred_element_type=jnp.float32)


def local(activations, out_grad, expert_ids, gate_values, w_gate, w_up, w_down):
    experts = lax.axis_size("ep")
    tokens, width = activations.shape
    lanes = (width // 128, 128)
    swap = lambda a: lax.ppermute(a, "grp", [(0, 1), (1, 0)])
    exchange = lambda a: lax.all_to_all(a, "ep", split_axis=0, concat_axis=0, tiled=True)

    send_x, place = fill_x(expert_ids.T, activations.reshape((tokens,) + lanes), experts)
    send_dy = fill_dy(
        place, gate_values.T.astype(jnp.float32), out_grad.reshape((tokens,) + lanes), experts
    )
    gate_w = jnp.concatenate([w_gate[0], swap(w_gate[0])], axis=1)
    up_w = jnp.concatenate([w_up[0], swap(w_up[0])], axis=1)
    down_w = jnp.concatenate([w_down[0], swap(w_down[0])], axis=0)

    arrived_x, send_dy = lax.optimization_barrier((exchange(send_x), send_dy))
    x = arrived_x.reshape(-1, width)
    pre_gate = contract(x, gate_w, ((1,), (0,)))
    pre_up = contract(x, up_w, ((1,), (0,)))
    sig = jax.nn.sigmoid(pre_gate)
    silu = pre_gate * sig
    slope = pre_up * sig * (1.0 + pre_gate * (1.0 - sig))
    weighted = (silu * pre_up).astype(jnp.bfloat16)
    slope, silu, weighted = lax.optimization_barrier((slope, silu, weighted))

    arrived_dy = exchange(send_dy)
    row_grad, grad_pre_gate, grad_pre_up = row_grads(arrived_dy, slope, silu, down_w, gate_w, up_w)
    returned = exchange(row_grad)

    half = w_gate.shape[2]
    dy = arrived_dy.reshape(-1, width)
    rows_t = ((0,), (0,))
    theirs = swap(
        (
            contract(x, grad_pre_gate[:, half:], rows_t).astype(jnp.bfloat16),
            contract(x, grad_pre_up[:, half:], rows_t).astype(jnp.bfloat16),
            contract(weighted[:, half:], dy, rows_t).astype(jnp.bfloat16),
        )
    )
    mine = (
        contract(x, grad_pre_gate[:, :half], rows_t),
        contract(x, grad_pre_up[:, :half], rows_t),
        contract(weighted[:, :half], dy, rows_t),
    )
    grads = [(m + t.astype(jnp.float32)).astype(jnp.bfloat16)[None] for m, t in zip(mine, theirs)]
    grad_input = combine(place, returned, tokens).reshape(tokens, width)
    return (grad_input, *grads)


def solution(mesh):
    tokens = P(("grp", "ep"), None)
    columns, rows = P("ep", None, "grp"), P("ep", "grp", None)
    return jax.shard_map(
        local,
        mesh=mesh,
        in_specs=(tokens, tokens, tokens, tokens, columns, columns, rows),
        out_specs=(tokens, columns, columns, rows),
        check_vma=False,
    )
```

time: 252 us -> 250 us (level)
  blocking collectives: 79.2 us -> 0 us
  waiting for transfers between devices: 101 us -> 154 us
  starting transfers between devices: 15.4 us -> 30.8 us
  matrix products: 39.8 us -> 24.7 us
  Pallas kernels: 7.12 us -> 19.9 us
  local copies, waits for them, and re-layouts: 7.38 us -> 13.2 us
  other arithmetic: 0 us -> 5.6 us
    all_to_all x1 -> x0, blocking collectives: 79.2 us -> none  [local(): lax.all_to_all(a, 'ep', split_axis=0, concat_axis=0, tiled=True)]
    all_to_all x2 -> x3, waiting for transfers between devices: 97 us -> 150 us  [local(): lax.all_to_all(a, 'ep', split_axis=0, concat_axis=0, tiled=True)]
    all_to_all x2 -> x3, starting transfers between devices: 14 us -> 29.1 us  [local(): lax.all_to_all(a, 'ep', split_axis=0, concat_axis=0, tiled=True)]
    dot_general x11 -> x8, matrix products: 39.8 us -> 24.7 us  [contract(): lax.dot_general(left, right, (dims, ((), ())), preferred_element_type=jnp...]
    pallas_call x1 -> x3, Pallas kernels: 5.55 us -> 18.2 us  [the longest x1 9.31 us: row_grads(): pl.pallas_call(functools.partial(row_grads_kernel, 2, 4), out_shape=(jax....]
    unnamed x29 -> x39, local copies, waits for them, and re-layouts: 6.37 us -> 13.2 us
    concatenate x0 -> x3, other arithmetic: none -> 5.6 us  [the longest x1 1.93 us: local(): up_w = jnp.concatenate([w_up[0], swap(w_up[0])], axis=1)]
  transfers between devices with their start and end apart: 8 -> 9, of which waited for: 3 -> 6; matrix products, arithmetic and copies ran while one was open for 11% -> 12% of each run, Pallas kernels for 0% -> 1%
where the time goes in v2:
time: 250 us; the launch traced here: 249 us
  waiting for transfers between devices  154 us (62%)
  starting transfers between devices  30.8 us (12%)
  matrix products  24.7 us (10%)
  Pallas kernels  19.9 us (8%)
  local copies, waits for them, and re-layouts  13.2 us (5%)
  other arithmetic  5.6 us (2%)
    all_to_all x3, waiting for transfers between devices, local(): lax.all_to_all(a, 'ep', split_axis=0, concat_axis=0, tiled=True)  150 us
    all_to_all x3, starting transfers between devices, local(): lax.all_to_all(a, 'ep', split_axis=0, concat_axis=0, tiled=True)  29.1 us
    dot_general x8, matrix products, contract(): lax.dot_general(left, right, (dims, ((), ())), preferred_element_type=jnp...  24.7 us
    unnamed x39, local copies, waits for them, and re-layouts  13.2 us
    pallas_call x1, Pallas kernels, row_grads(): pl.pallas_call(functools.partial(row_grads_kernel, 2, 4), out_shape=(jax....  9.31 us
    pallas_call x1, Pallas kernels, fill_x(): pl.pallas_call(fill_x_kernel, out_shape=(jax.ShapeDtypeStruct((experts *...  5.17 us
  transfers between devices with their start and end apart: 9, of which 6 were waited for; matrix products, arithmetic and copies ran while one was open for 12% of the time, Pallas kernels for 1%

profile of v2, /device:TPU:32, one launch (start us, length us, event | category | flops | bytes accessed | tf_op | source)
XLA Modules:
  0.0 249.3 jit_solution(14287224261913926277)
XLA Ops:
  2.5 5.2 %fill_x.1 = (bf16[640,16,128]{2,1,0:T(8,128)(2,1)}, s32[4,128]{1,0:T(4,128)S(1)}) custom-call(s32[4,128]{1,0:T(4,128)S(1)} %bitcast.57, bf16[128,16,128]{2,1,0:T(8,128)(2,1)S(1)} %bitcast.54), custom_call_target="tpu_custom_call" | custom-call | tf_op jit(solution)/shard_map/fill_x/pallas_call | solution.py:53
  7.7 15.2 %all-to-all-start = ((bf16[640,16,128]{2,1,0:T(8,128)(2,1)}), bf16[640,16,128]{2,1,0:T(8,128)(2,1)S(1)}, u32[]{:S(2)}, u32[]{:S(2)}) async-start(bf16[640,16,128]{2,1,0:T(8,128)(2,1)} %get-tuple-element.15), calls=%async_computation | async-start | bytes 5242880 | tf_op jit(solution)/shard_map/all_to_all | solution.py:142
  23.0 3.7 %fill_dy.1 = bf16[640,16,128]{2,1,0:T(8,128)(2,1)} custom-call(s32[4,128]{1,0:T(4,128)S(1)} %get-tuple-element.14.place, f32[4,128]{1,0:T(4,128)S(1)} %convert_bitcast_fusion.gates, bf16[128,16,128]{2,1,0:T(8,128)(2,1)S(1)} %bitcast.55), custom_call_target="tpu_custom_call" | custom-call | flops 10000000 | bytes 8388608 | tf_op jit(solution)/shard_map/fill_dy/pallas_call | solution.py:68
  26.7 60.5 %all-to-all-done = bf16[640,16,128]{2,1,0:T(8,128)(2,1)S(1)} async-done(((bf16[640,16,128]{2,1,0:T(8,128)(2,1)}), bf16[640,16,128]{2,1,0:T(8,128)(2,1)S(1)}, u32[]{:S(2)}, u32[]{:S(2)}) %all-to-all-start) | async-done | bytes 2621472 | tf_op jit(solution)/shard_map/all_to_all | solution.py:142
  87.2 7.1 %all-to-all-start.1 = ((bf16[640,16,128]{2,1,0:T(8,128)(2,1)}), bf16[640,16,128]{2,1,0:T(8,128)(2,1)}, u32[]{:S(2)}, u32[]{:S(2)}) async-start(bf16[640,16,128]{2,1,0:T(8,128)(2,1)} %fill_dy.1), calls=%async_computation.1 | async-start | bytes 5242880 | tf_op jit(solution)/shard_map/all_to_all | solution.py:142
  95.1 3.0 %collective-permute-done.2 = bf16[384,2048]{1,0:T(8,128)(2,1)S(1)} collective-permute-done((bf16[384,2048]{1,0:T(8,128)(2,1)}, bf16[384,2048]{1,0:T(8,128)(2,1)S(1)}, u32[]{:S(2)}, u32[]{:S(2)}) %collective-permute-start.2) | collective-permute-done | bytes 1572896 | tf_op jit(solution)/shard_map/ppermute | solution.py:141
  98.1 1.8 pad_maximum_fusion.2.w_down
  100.3 1.9 pad_maximum_fusion.1.w_gate
  102.6 1.9 pad_maximum_fusion.w_up
  104.5 2.2 fusion.11
  106.7 5.1 %multiply_convert_fusion = (bf16[640,768]{1,0:T(8,128)(2,1)}, f32[640,768]{1,0:T(8,128)}, f32[640,768]{1,0:T(8,128)}) fusion(f32[640,768]{1,0:T(8,128)S(1)} %fusion.11, bf16[2048,384]{1,0:T(8,128)(2,1)S(1)} %collective-permute-done, bf16[2048,384]{1,0:T(8,128)(2,1)S(1)} %bitcast.71, bf16[80,8,16,128]{3,2,1,0:T(8,128)(2,1)S(1)} %bitcast.59), kind=kOutput, calls=%fused_computation.27 | convolution fusion | flops 2024964096 | bytes 12648448 | tf_op jit(solution)/shard_map/dot_general | solution.py:134
  111.8 45.7 %all-to-all-done.1.dy = bf16[640,16,128]{2,1,0:T(8,128)(2,1)} async-done(((bf16[640,16,128]{2,1,0:T(8,128)(2,1)}), bf16[640,16,128]{2,1,0:T(8,128)(2,1)}, u32[]{:S(2)}, u32[]{:S(2)}) %all-to-all-start.1) | async-done | bytes 2621472 | tf_op jit(solution)/shard_map/all_to_all | solution.py:142
  157.5 1.9 copy-done
  159.4 1.9 copy-done.1
  164.4 9.3 %row_grads.1 = (bf16[640,16,128]{2,1,0:T(8,128)(2,1)S(1)}, bf16[640,768]{1,0:T(8,128)(2,1)S(1)}, bf16[640,768]{1,0:T(8,128)(2,1)S(1)}) custom-call(bf16[640,16,128]{2,1,0:T(8,128)(2,1)} %all-to-all-done.1.dy, f32[640,768]{1,0:T(8,128)S(1)} %copy-done.4, f32[640,768]{1,0:T(8,128)S(1)} %copy-done.5, bf16[768,2048]{1,0:T(8,128)(2,1)S(1)} %pad_maximum_fusion.2.w_down, ...), custom_call_target="tpu_custom_call" | custom-call | flops 6039797760 | bytes 8388608 | tf_op jit(solution)/shard_map/row_grads/pallas_call | solution.py:98
  177.1 6.8 %all-to-all-start.2 = ((bf16[640,16,128]{2,1,0:T(8,128)(2,1)}), bf16[640,16,128]{2,1,0:T(8,128)(2,1)S(1)}, u32[]{:S(2)}, u32[]{:S(2)}) async-start(bf16[640,16,128]{2,1,0:T(8,128)(2,1)} %copy-done.2), calls=%async_computation.2 | async-start | bytes 5242880 | tf_op jit(solution)/shard_map/all_to_all | solution.py:142
  184.0 3.5 %convolution_convert_fusion = bf16[384,2048]{1,0:T(8,128)(2,1)S(1)} fusion(bf16[80,8,16,128]{3,2,1,0:T(8,128)(2,1)} %bitcast.16, bf16[640,768]{1,0:T(8,128)(2,1)} %get-tuple-element.23), kind=kOutput, calls=%fused_computation.6 | convolution fusion | flops 1007419392 | bytes 4685824 | tf_op jit(solution)/shard_map/dot_general | solution.py:134
  187.6 1.8 convolution_convert_fusion.2
  189.9 1.8 convolution_convert_fusion.1
  192.1 4.4 %fusion.25 = bf16[1,384,2048]{2,1,0:T(8,128)(2,1)} fusion(bf16[384,2048]{1,0:T(8,128)(2,1)S(1)} %collective-permute-done.5, bf16[80,8,16,128]{3,2,1,0:T(8,128)(2,1)} %bitcast.16, bf16[640,768]{1,0:T(8,128)(2,1)S(1)} %copy-done.17), kind=kOutput, calls=%fused_computation.24 | convolution fusion | flops 1008992256 | bytes 6258688 | tf_op jit(solution)/shard_map/dot_general | solution.py:134
  196.5 3.0 %fusion.19 = bf16[1,2048,384]{2,1,0:T(8,128)(2,1)} fusion(bf16[2048,384]{1,0:T(8,128)(2,1)S(1)} %collective-permute-done.3, bf16[80,8,16,128]{3,2,1,0:T(8,128)(2,1)S(1)} %bitcast.62, bf16[640,768]{1,0:T(8,128)(2,1)S(1)} %copy-done.9), kind=kOutput, calls=%fused_computation.22 | convolution fusion | flops 1008992256 | bytes 6258688 | tf_op jit(solution)/shard_map/dot_general | solution.py:134
  199.5 3.0 %fusion.22 = bf16[1,2048,384]{2,1,0:T(8,128)(2,1)} fusion(bf16[2048,384]{1,0:T(8,128)(2,1)S(1)} %collective-permute-done.4, bf16[80,8,16,128]{3,2,1,0:T(8,128)(2,1)S(1)} %bitcast.63, bf16[640,768]{1,0:T(8,128)(2,1)S(1)} %copy-done.7), kind=kOutput, calls=%fused_computation.23 | convolution fusion | flops 1008992256 | bytes 6258688 | tf_op jit(solution)/shard_map/dot_general | solution.py:134
  202.5 44.1 %all-to-all-done.2.rows = bf16[640,16,128]{2,1,0:T(8,128)(2,1)S(1)} async-done(((bf16[640,16,128]{2,1,0:T(8,128)(2,1)}), bf16[640,16,128]{2,1,0:T(8,128)(2,1)S(1)}, u32[]{:S(2)}, u32[]{:S(2)}) %all-to-all-start.2) | async-done | bytes 2621472 | tf_op jit(solution)/shard_map/all_to_all | solution.py:142
  246.6 1.8 combine.1
  (49 shorter events, 11.9 us)
Async XLA Ops:
  7.6 15.2 %copy-start.15 = (bf16[128,2048]{1,0:T(8,128)(2,1)S(1)}, bf16[128,2048]{1,0:T(8,128)(2,1)}, u32[]{:S(2)}) copy-start(bf16[128,2048]{1,0:T(8,128)(2,1)} %param.8) | copy-start | bytes 1572868
  7.7 15.3 %copy-start.16 = (bf16[128,4]{0,1:T(4,128)(2,1)S(1)}, bf16[128,4]{0,1:T(4,128)(2,1)}, u32[]{:S(2)}) copy-start(bf16[128,4]{0,1:T(4,128)(2,1)} %param.10) | copy-start | bytes 3076
  7.7 79.5 %all-to-all-start = ((bf16[640,16,128]{2,1,0:T(8,128)(2,1)}), bf16[640,16,128]{2,1,0:T(8,128)(2,1)S(1)}, u32[]{:S(2)}, u32[]{:S(2)}) async-start(bf16[640,16,128]{2,1,0:T(8,128)(2,1)} %get-tuple-element.15), calls=%async_computation | async-start | bytes 5242880 | tf_op jit(solution)/shard_map/all_to_all | solution.py:142
  87.2 7.1 %copy-start.10 = (bf16[640,16,128]{2,1,0:T(8,128)(2,1)}, bf16[640,16,128]{2,1,0:T(8,128)(2,1)S(1)}, u32[]{:S(2)}) copy-start(bf16[640,16,128]{2,1,0:T(8,128)(2,1)S(1)} %all-to-all-done) | copy-start | bytes 7864324
  87.2 70.3 %all-to-all-start.1 = ((bf16[640,16,128]{2,1,0:T(8,128)(2,1)}), bf16[640,16,128]{2,1,0:T(8,128)(2,1)}, u32[]{:S(2)}, u32[]{:S(2)}) async-start(bf16[640,16,128]{2,1,0:T(8,128)(2,1)} %fill_dy.1), calls=%async_computation.1 | async-start | bytes 5242880 | tf_op jit(solution)/shard_map/all_to_all | solution.py:142
  94.3 3.7 %collective-permute-start.2 = (bf16[384,2048]{1,0:T(8,128)(2,1)}, bf16[384,2048]{1,0:T(8,128)(2,1)S(1)}, u32[]{:S(2)}, u32[]{:S(2)}) collective-permute-start(bf16[384,2048]{1,0:T(8,128)(2,1)} %bitcast.64), channel_id=1, source_target_pairs={{0,128},{128,0},{1,129},{129,1},{2,130},{130,2},{3,131},{131,3},{4... | collective-permute-start | bytes 4718600 | tf_op jit(solution)/shard_map/ppermute | solution.py:141
  94.5 5.9 %collective-permute-start.1 = (bf16[2048,384]{1,0:T(8,128)(2,1)}, bf16[2048,384]{1,0:T(8,128)(2,1)S(1)}, u32[]{:S(2)}, u32[]{:S(2)}) collective-permute-start(bf16[2048,384]{1,0:T(8,128)(2,1)} %bitcast.66), channel_id=1, source_target_pairs={{0,128},{128,0},{1,129},{129,1},{2,130},{130,2},{3,131},{131,3},{4... | collective-permute-start | bytes 4718600 | tf_op jit(solution)/shard_map/ppermute | solution.py:141
  94.9 5.4 %copy-start.13 = (bf16[1,2048,384]{2,1,0:T(8,128)(2,1)S(1)}, bf16[1,2048,384]{2,1,0:T(8,128)(2,1)}, u32[]{:S(2)}) copy-start(bf16[1,2048,384]{2,1,0:T(8,128)(2,1)} %param.11) | copy-start | bytes 4718596
  94.9 7.6 %collective-permute-start = (bf16[2048,384]{1,0:T(8,128)(2,1)}, bf16[2048,384]{1,0:T(8,128)(2,1)S(1)}, u32[]{:S(2)}, u32[]{:S(2)}) collective-permute-start(bf16[2048,384]{1,0:T(8,128)(2,1)} %bitcast.69), channel_id=1, source_target_pairs={{0,128},{128,0},{1,129},{129,1},{2,130},{130,2},{3,131},{131,3},{4... | collective-permute-start | bytes 4718600 | tf_op jit(solution)/shard_map/ppermute | solution.py:141
  99.8 2.7 %copy-start.14 = (bf16[1,2048,384]{2,1,0:T(8,128)(2,1)S(1)}, bf16[1,2048,384]{2,1,0:T(8,128)(2,1)}, u32[]{:S(2)}) copy-start(bf16[1,2048,384]{2,1,0:T(8,128)(2,1)} %param.12) | copy-start | bytes 4718596
  102.2 2.3 copy-start.11
  157.5 1.9 copy-start
  159.4 1.9 copy-start.1
  161.3 1.5 copy-start.4
  162.8 1.5 copy-start.5
  173.7 1.5 copy-start.2
  177.1 69.5 %all-to-all-start.2 = ((bf16[640,16,128]{2,1,0:T(8,128)(2,1)}), bf16[640,16,128]{2,1,0:T(8,128)(2,1)S(1)}, u32[]{:S(2)}, u32[]{:S(2)}) async-start(bf16[640,16,128]{2,1,0:T(8,128)(2,1)} %copy-done.2), calls=%async_computation.2 | async-start | bytes 5242880 | tf_op jit(solution)/shard_map/all_to_all | solution.py:142
  183.9 3.6 %copy-start.9 = (bf16[640,768]{1,0:T(8,128)(2,1)S(1)}, bf16[640,768]{1,0:T(8,128)(2,1)}, u32[]{:S(2)}) copy-start(bf16[640,768]{1,0:T(8,128)(2,1)} %copy-done.8) | copy-start | bytes 2949124
  184.0 3.6 %copy-start.12 = (bf16[640,16,128]{2,1,0:T(8,128)(2,1)S(1)}, bf16[640,16,128]{2,1,0:T(8,128)(2,1)}, u32[]{:S(2)}) copy-start(bf16[640,16,128]{2,1,0:T(8,128)(2,1)} %copy-done.10) | copy-start | bytes 7864324
  187.5 4.7 %collective-permute-start.5 = (bf16[384,2048]{1,0:T(8,128)(2,1)S(1)}, bf16[384,2048]{1,0:T(8,128)(2,1)S(1)}, u32[]{:S(2)}, u32[]{:S(2)}) collective-permute-start(bf16[384,2048]{1,0:T(8,128)(2,1)S(1)} %convolution_convert_fusion), channel_id=1, source_target_pairs={{0,128},{128,0},{1,129},{129,1},{2,130},{130,2},{3,131},{131,3},{4... | collective-permute-start | bytes 4718600 | tf_op jit(solution)/shard_map/ppermute | solution.py:141
  187.6 2.4 copy-start.7
  189.4 7.1 %collective-permute-start.3 = (bf16[2048,384]{1,0:T(8,128)(2,1)S(1)}, bf16[2048,384]{1,0:T(8,128)(2,1)S(1)}, u32[]{:S(2)}, u32[]{:S(2)}) collective-permute-start(bf16[2048,384]{1,0:T(8,128)(2,1)S(1)} %convolution_convert_fusion.2), channel_id=1, source_target_pairs={{0,128},{128,0},{1,129},{129,1},{2,130},{130,2},{3,131},{131,3},{4... | collective-permute-start | bytes 4718600 | tf_op jit(solution)/shard_map/ppermute | solution.py:141
  189.9 2.2 copy-start.17
  191.7 7.8 %collective-permute-start.4 = (bf16[2048,384]{1,0:T(8,128)(2,1)S(1)}, bf16[2048,384]{1,0:T(8,128)(2,1)S(1)}, u32[]{:S(2)}, u32[]{:S(2)}) collective-permute-start(bf16[2048,384]{1,0:T(8,128)(2,1)S(1)} %convolution_convert_fusion.1), channel_id=1, source_target_pairs={{0,128},{128,0},{1,129},{129,1},{2,130},{130,2},{3,131},{131,3},{4... | collective-permute-start | bytes 4718600 | tf_op jit(solution)/shard_map/ppermute | solution.py:141
  (3 other events, 2.6 us)

commit v3 on v1

v3 whole, which is shorter than its diff:
```python
import functools

import jax
import jax.numpy as jnp
from jax import lax
from jax.experimental import pallas as pl
from jax.experimental.pallas import tpu as pltpu
from jax.sharding import PartitionSpec as P

CAP = 5
VMEM = pl.BlockSpec(memory_space=pltpu.VMEM)
ANY = pl.BlockSpec(memory_space=pl.ANY)
SMEM = pl.BlockSpec(memory_space=pltpu.SMEM)


def fill_kernel(ids, gates, x, dy, out, place, send, count, sem):
    top, tokens = ids.shape

    def clear_count(e, carry):
        count[e] = 0
        return carry

    lax.fori_loop(0, count.shape[0], clear_count, 0, unroll=8)
    send[...] = jnp.zeros_like(send)

    def one_token(t, carry):
        x_row = x[t]
        dy_row = dy[t].astype(jnp.float32)
        for k in range(top):
            expert = ids[k, t]
            taken = count[expert]
            count[expert] = taken + 1
            place[k, t] = expert * CAP + taken
            slot = expert * (2 * CAP) + taken
            send[slot] = x_row
            send[slot + CAP] = (dy_row * gates[k, t]).astype(jnp.bfloat16)
        return carry

    lax.fori_loop(0, tokens, one_token, 0, unroll=4)
    done = pltpu.make_async_copy(send, out, sem)
    done.start()
    done.wait()


def fill_slots(ids, gates, x, dy, experts):
    shape = (experts * 2 * CAP,) + x.shape[1:]
    return pl.pallas_call(
        fill_kernel,
        out_shape=(jax.ShapeDtypeStruct(shape, x.dtype), jax.ShapeDtypeStruct(ids.shape, jnp.int32)),
        in_specs=[SMEM, SMEM, VMEM, VMEM],
        out_specs=(ANY, SMEM),
        scratch_shapes=[
            pltpu.VMEM(shape, x.dtype),
            pltpu.SMEM((experts,), jnp.int32),
            pltpu.SemaphoreType.DMA,
        ],
        compiler_params=pltpu.CompilerParams(vmem_limit_bytes=58 * 2**20),
        name="fill_slots",
    )(ids, gates, x, dy)


def row_grads_kernel(
    parts, columns, arrived, gate_a, gate_b, up_a, up_b, down_a, down_b,
    out, weighted, grad_gate, grad_up,
    v_x, v_dy, v_gate, v_up, v_down, v_out, v_weighted, v_grad_gate, v_grad_up,
    x_sem, dy_sem, w_sem, out_sem,
):
    sources, _, blocks, lanes = arrived.shape
    half, width = down_a.shape
    some = sources // parts
    step, group = some * CAP, blocks // columns
    copy = pltpu.make_async_copy
    sides = (pl.ds(0, half), pl.ds(half, half))
    x_in, dy_in = [], []
    for i in range(parts):
        s = pl.ds(i * some, some)
        x_in.append(copy(arrived.at[s, pl.ds(0, CAP)], v_x.at[s], x_sem.at[i]))
        dy_in.append(copy(arrived.at[s, pl.ds(CAP, CAP)], v_dy.at[s], dy_sem.at[i]))
    gate_in = [copy(w, v_gate.at[:, d], w_sem.at[0 + j]) for j, (w, d) in enumerate(zip((gate_a, gate_b), sides))]
    up_in = [copy(w, v_up.at[:, d], w_sem.at[2 + j]) for j, (w, d) in enumerate(zip((up_a, up_b), sides))]
    down_in = [copy(w, v_down.at[d], w_sem.at[4 + j]) for j, (w, d) in enumerate(zip((down_a, down_b), sides))]
    for c in [x_in[0], *gate_in, *up_in, dy_in[0], *down_in]:
        c.start()
    for i in range(1, parts):
        x_in[i].start()
        dy_in[i].start()

    outs = []
    for i in range(parts):
        s, r = pl.ds(i * some, some), pl.ds(i * step, step)
        x_in[i].wait()
        x = v_x[s].reshape(step, width)
        if i == 0:
            for c in gate_in:
                c.wait()
        pre_gate = contract(x, v_gate[...], ((1,), (0,)))
        if i == 0:
            for c in up_in:
                c.wait()
        pre_up = contract(x, v_up[...], ((1,), (0,)))
        sig = jax.nn.sigmoid(pre_gate)
        silu = pre_gate * sig
        v_weighted[r, :] = (silu * pre_up).astype(jnp.bfloat16)
        dy_in[i].wait()
        if i == 0:
            for c in down_in:
                c.wait()
        grad_hidden = contract(v_dy[s].reshape(step, width), v_down[...], ((1,), (1,)))
        slope = pre_up * sig * (1.0 + pre_gate * (1.0 - sig))
        v_grad_gate[r, :] = (grad_hidden * slope).astype(jnp.bfloat16)
        v_grad_up[r, :] = (grad_hidden * silu).astype(jnp.bfloat16)
        for c in range(columns):
            w = pl.ds(c * group * lanes, group * lanes)
            total = contract(v_grad_gate[r, :], v_gate[w, :], ((1,), (1,)))
            total = total + contract(v_grad_up[r, :], v_up[w, :], ((1,), (1,)))
            v_out[r, pl.ds(c * group, group), :] = total.astype(jnp.bfloat16).reshape(step, group, lanes)
        pairs = ((v_out, out), (v_weighted, weighted), (v_grad_gate, grad_gate), (v_grad_up, grad_up))
        for j, (v, o) in enumerate(pairs):
            outs.append(copy(v.at[r], o.at[r], out_sem.at[4 * i + j]))
            outs[-1].start()
    for c in outs:
        c.wait()


def row_grads(arrived, gate_a, gate_b, up_a, up_b, down_a, down_b, parts=2, columns=2):
    sources, _, blocks, lanes = arrived.shape
    half, width = down_a.shape
    rows, hidden = sources * CAP, 2 * half
    struct = lambda *shape: jax.ShapeDtypeStruct(shape, jnp.bfloat16)
    vmem = lambda *shape: pltpu.VMEM(shape, jnp.bfloat16)
    dma = lambda n: pltpu.SemaphoreType.DMA((n,))
    return pl.pallas_call(
        functools.partial(row_grads_kernel, parts, columns),
        out_shape=(struct(rows, blocks, lanes),) + (struct(rows, hidden),) * 3,
        in_specs=[ANY] * 7,
        out_specs=(ANY,) * 4,
        scratch_shapes=[
            vmem(sources, CAP, blocks, lanes), vmem(sources, CAP, blocks, lanes),
            vmem(width, hidden), vmem(width, hidden), vmem(hidden, width),
            vmem(rows, blocks, lanes), vmem(rows, hidden), vmem(rows, hidden), vmem(rows, hidden),
            dma(parts), dma(parts), dma(6), dma(4 * parts),
        ],
        compiler_params=pltpu.CompilerParams(vmem_limit_bytes=58 * 2**20),
        cost_estimate=pl.CostEstimate(
            flops=10 * rows * hidden * width, bytes_accessed=24 * 2**20, transcendentals=rows * hidden
        ),
        name="row_grads",
    )(arrived, gate_a, gate_b, up_a, up_b, down_a, down_b)


def combine_kernel(place, rows, out):
    def one_token(t, carry):
        total = rows[place[0, t]].astype(jnp.float32)
        for k in range(1, place.shape[0]):
            total = total + rows[place[k, t]].astype(jnp.float32)
        out[t] = total.astype(jnp.bfloat16)
        return carry

    lax.fori_loop(0, out.shape[0], one_token, 0, unroll=2)


def combine(place, rows, tokens):
    return pl.pallas_call(
        combine_kernel,
        out_shape=jax.ShapeDtypeStruct((tokens,) + rows.shape[1:], jnp.bfloat16),
        in_specs=[SMEM, VMEM],
        out_specs=VMEM,
        compiler_params=pltpu.CompilerParams(vmem_limit_bytes=16 * 2**20),
        name="combine",
    )(place, rows)


def contract(left, right, dims):
    return lax.dot_general(left, right, (dims, ((), ())), preferred_element_type=jnp.float32)


def local(activations, out_grad, expert_ids, gate_values, w_gate, w_up, w_down):
    experts = lax.axis_size("ep")
    tokens, width = activations.shape
    lanes = (width // 128, 128)
    swap = lambda a: lax.ppermute(a, "grp", [(0, 1), (1, 0)])
    exchange = lambda a: lax.all_to_all(a, "ep", split_axis=0, concat_axis=0, tiled=True)

    send, place = fill_slots(
        expert_ids.T,
        gate_values.T.astype(jnp.float32),
        activations.reshape((tokens,) + lanes),
        out_grad.reshape((tokens,) + lanes),
        experts,
    )
    weights = []
    for w in (w_gate[0], w_up[0], w_down[0]):
        weights += [w, swap(w)]
    arrived = exchange(send).reshape((experts, 2 * CAP) + lanes)
    row_grad, weighted, grad_pre_gate, grad_pre_up = row_grads(arrived, *weights)
    returned = exchange(row_grad)

    half = w_gate.shape[2]
    x, dy = (arrived[:, i * CAP : (i + 1) * CAP].reshape(-1, width) for i in range(2))
    rows_t = ((0,), (0,))
    theirs = swap(
        (
            contract(x, grad_pre_gate[:, half:], rows_t).astype(jnp.bfloat16),
            contract(x, grad_pre_up[:, half:], rows_t).astype(jnp.bfloat16),
            contract(weighted[:, half:], dy, rows_t).astype(jnp.bfloat16),
        )
    )
    mine = (
        contract(x, grad_pre_gate[:, :half], rows_t),
        contract(x, grad_pre_up[:, :half], rows_t),
        contract(weighted[:, :half], dy, rows_t),
    )
    grads = [(m + t.astype(jnp.float32)).astype(jnp.bfloat16)[None] for m, t in zip(mine, theirs)]
    grad_input = combine(place, returned, tokens).reshape(tokens, width)
    return (grad_input, *grads)


def solution(mesh):
    tokens = P(("grp", "ep"), None)
    columns, rows = P("ep", None, "grp"), P("ep", "grp", None)
    return jax.shard_map(
        local,
        mesh=mesh,
        in_specs=(tokens, tokens, tokens, tokens, columns, columns, rows),
        out_specs=(tokens, columns, columns, rows),
        check_vma=False,
    )
```

time: 252 us -> 242 us (0.960)
  blocking collectives: 79.2 us -> 0 us
  waiting for transfers between devices: 101 us -> 162 us
  matrix products: 39.8 us -> 13.7 us
  Pallas kernels: 7.12 us -> 28.4 us
  starting transfers between devices: 15.4 us -> 25.9 us
    all_to_all x1 -> x0, blocking collectives: 79.2 us -> none  [local(): lax.all_to_all(a, 'ep', split_axis=0, concat_axis=0, tiled=True)]
    all_to_all x2, waiting for transfers between devices: 97 us -> 155 us  [local(): lax.all_to_all(a, 'ep', split_axis=0, concat_axis=0, tiled=True)]
    dot_general x11 -> x6, matrix products: 39.8 us -> 13.7 us  [contract(): lax.dot_general(left, right, (dims, ((), ())), preferred_element_type=jnp...]
    pallas_call x1 -> x2, Pallas kernels: 5.55 us -> 26.6 us  [the longest x1 18.6 us: row_grads(): pl.pallas_call(functools.partial(row_grads_kernel, parts, columns), out_s...]
    all_to_all x2, starting transfers between devices: 14 us -> 24.2 us  [local(): lax.all_to_all(a, 'ep', split_axis=0, concat_axis=0, tiled=True)]
    slice x0 -> x1, local copies, waits for them, and re-layouts: none -> 3.54 us  [local(): arrived[:, i * CAP:(i + 1) * CAP].reshape(-1, width)]
    ppermute x6, waiting for transfers between devices: 4.24 us -> 7.3 us  [local(): swap = lambda a: lax.ppermute(a, 'grp', [(0, 1), (1, 0)])]
    unnamed x29 -> x19, local copies, waits for them, and re-layouts: 6.37 us -> 6 us
  transfers between devices with their start and end apart: 8 -> 8, of which waited for: 3 -> 4; matrix products, arithmetic and copies ran while one was open for 11% -> 7% of each run, Pallas kernels for 0% -> 0%
where the time goes in v3:
time: 242 us
  waiting for transfers between devices  162 us (67%)
  Pallas kernels  28.4 us (12%)
  starting transfers between devices  25.9 us (11%)
  matrix products  13.7 us (6%)
  local copies, waits for them, and re-layouts  9.54 us (4%)
    all_to_all x2, waiting for transfers between devices, local(): lax.all_to_all(a, 'ep', split_axis=0, concat_axis=0, tiled=True)  155 us
    all_to_all x2, starting transfers between devices, local(): lax.all_to_all(a, 'ep', split_axis=0, concat_axis=0, tiled=True)  24.2 us
    pallas_call x1, Pallas kernels, row_grads(): pl.pallas_call(functools.partial(row_grads_kernel, parts, columns), out_s...  18.6 us
    dot_general x6, matrix products, contract(): lax.dot_general(left, right, (dims, ((), ())), preferred_element_type=jnp...  13.7 us
    pallas_call x1, Pallas kernels, fill_slots(): pl.pallas_call(fill_kernel, out_shape=(jax.ShapeDtypeStruct(shape, x.dtyp...  8 us
    ppermute x6, waiting for transfers between devices, local(): swap = lambda a: lax.ppermute(a, 'grp', [(0, 1), (1, 0)])  7.3 us
    unnamed x19, local copies, waits for them, and re-layouts  6 us
  transfers between devices with their start and end apart: 8, of which 4 were waited for; matrix products, arithmetic and copies ran while one was open for 7% of the time, Pallas kernels for 0%

profile of v3, /device:TPU:32, one launch (start us, length us, event | category | flops | bytes accessed | tf_op | source)
XLA Modules:
  0.0 242.0 jit_solution(14636649760549985127)
XLA Ops:
  0.6 1.3 convert_bitcast_fusion.gates
  1.9 1.9 copy.11
  3.8 1.9 copy.12
  5.8 8.0 %fill_slots.1 = (bf16[1280,16,128]{2,1,0:T(8,128)(2,1)}, s32[4,128]{1,0:T(4,128)}) custom-call(s32[4,128]{1,0:T(4,128)} %bitcast.57, f32[4,128]{1,0:T(4,128)} %convert_bitcast_fusion.gates, bf16[128,16,128]{2,1,0:T(8,128)(2,1)} %bitcast.52, bf16[128,16,128]{2,1,0:T(8,128)(2,1)} %bitcast.53), custom_call_target="tpu_custom_call" | custom-call | tf_op jit(solution)/shard_map/fill_slots/pallas_call | solution.py:47
  13.8 15.7 %all-to-all-start = ((bf16[1280,16,128]{2,1,0:T(8,128)(2,1)}), bf16[1280,16,128]{2,1,0:T(8,128)(2,1)}, u32[]{:S(2)}, u32[]{:S(2)}) async-start(bf16[1280,16,128]{2,1,0:T(8,128)(2,1)} %get-tuple-element.11), calls=%async_computation | async-start | bytes 10485760 | tf_op jit(solution)/shard_map/all_to_all | solution.py:182
  29.6 0.5 collective-permute-start.1
  30.2 2.8 %collective-permute-done.gate_b = bf16[2048,384]{1,0:T(8,128)(2,1)S(1)} collective-permute-done((bf16[2048,384]{1,0:T(8,128)(2,1)S(1)}, bf16[2048,384]{1,0:T(8,128)(2,1)S(1)}, u32[]{:S(2)}, u32[]{:S(2)}) %collective-permute-start) | collective-permute-done | bytes 1572896 | tf_op jit(solution)/shard_map/ppermute | solution.py:181
  33.0 4.5 %collective-permute-done.1.up_b = bf16[2048,384]{1,0:T(8,128)(2,1)S(1)} collective-permute-done((bf16[2048,384]{1,0:T(8,128)(2,1)S(1)}, bf16[2048,384]{1,0:T(8,128)(2,1)S(1)}, u32[]{:S(2)}, u32[]{:S(2)}) %collective-permute-start.1) | collective-permute-done | bytes 1572896 | tf_op jit(solution)/shard_map/ppermute | solution.py:181
  37.5 1.1 copy-done.4
  38.7 109.2 %all-to-all-done = bf16[1280,16,128]{2,1,0:T(8,128)(2,1)} async-done(((bf16[1280,16,128]{2,1,0:T(8,128)(2,1)}), bf16[1280,16,128]{2,1,0:T(8,128)(2,1)}, u32[]{:S(2)}, u32[]{:S(2)}) %all-to-all-start) | async-done | bytes 5242912 | tf_op jit(solution)/shard_map/all_to_all | solution.py:182
  147.9 18.6 %row_grads.1 = (bf16[640,16,128]{2,1,0:T(8,128)(2,1)}, bf16[640,768]{1,0:T(8,128)(2,1)}, bf16[640,768]{1,0:T(8,128)(2,1)}, bf16[640,768]{1,0:T(8,128)(2,1)}) custom-call(bf16[128,10,16,128]{3,2,1,0:T(8,128)(2,1)} %bitcast.2.arrived, bf16[2048,384]{1,0:T(8,128)(2,1)} %bitcast.58, bf16[2048,384]{1,0:T(8,128)(2,1)} %copy-done.3, bf16[2048,384]{1,0:T(8,128)(2,1)} %bitcast.60, ...), custom_call_target="tpu_custom_call" | custom-call | flops 10066329600 | bytes 25165824 | tf_op jit(solution)/shard_map/row_grads/pallas_call | solution.py:132
  166.5 8.5 %all-to-all-start.1 = ((bf16[640,16,128]{2,1,0:T(8,128)(2,1)}), bf16[640,16,128]{2,1,0:T(8,128)(2,1)S(1)}, u32[]{:S(2)}, u32[]{:S(2)}) async-start(bf16[640,16,128]{2,1,0:T(8,128)(2,1)} %get-tuple-element.12), calls=%async_computation.1 | async-start | bytes 5242880 | tf_op jit(solution)/shard_map/all_to_all | solution.py:182
  175.1 3.5 %fusion.27 = (bf16[128,5,16,128]{3,2,1,0:T(8,128)(2,1)S(1)}, bf16[128,5,16,128]{3,2,1,0:T(8,128)(2,1)S(1)}) fusion(bf16[128,10,16,128]{3,2,1,0:T(8,128)(2,1)} %bitcast.2.arrived), kind=kLoop, calls=%fused_computation.29 | loop fusion | bytes 10485760 | tf_op jit(solution)/shard_map/slice | solution.py:199
  178.6 1.4 convolution_convert_fusion
  180.2 1.8 convolution_convert_fusion.2
  182.0 0.6 collective-permute-start.3
  182.6 1.8 convolution_convert_fusion.1
  184.4 0.4 collective-permute-start.4
  184.7 2.6 %fusion.12 = bf16[1,384,2048]{2,1,0:T(8,128)(2,1)} fusion(bf16[384,2048]{1,0:T(8,128)(2,1)S(1)} %collective-permute-done.5, bf16[80,8,16,128]{3,2,1,0:T(8,128)(2,1)S(1)} %bitcast.51, bf16[640,768]{1,0:T(8,128)(2,1)S(1)} %copy-done.5), kind=kOutput, calls=%fused_computation.14 | convolution fusion | flops 1008992256 | bytes 6258688 | tf_op jit(solution)/shard_map/dot_general | solution.py:174
  187.4 3.0 %fusion.6 = bf16[1,2048,384]{2,1,0:T(8,128)(2,1)} fusion(bf16[2048,384]{1,0:T(8,128)(2,1)S(1)} %collective-permute-done.3, bf16[80,8,16,128]{3,2,1,0:T(8,128)(2,1)S(1)} %bitcast.48, bf16[640,768]{1,0:T(8,128)(2,1)S(1)} %copy-done.7), kind=kOutput, calls=%fused_computation.12 | convolution fusion | flops 1008992256 | bytes 6258688 | tf_op jit(solution)/shard_map/dot_general | solution.py:174
  190.4 3.0 %fusion.9 = bf16[1,2048,384]{2,1,0:T(8,128)(2,1)} fusion(bf16[2048,384]{1,0:T(8,128)(2,1)S(1)} %collective-permute-done.4, bf16[80,8,16,128]{3,2,1,0:T(8,128)(2,1)S(1)} %bitcast.49, bf16[640,768]{1,0:T(8,128)(2,1)S(1)} %copy-done.6), kind=kOutput, calls=%fused_computation.13 | convolution fusion | flops 1008992256 | bytes 6258688 | tf_op jit(solution)/shard_map/dot_general | solution.py:174
  193.4 45.9 %all-to-all-done.1.rows = bf16[640,16,128]{2,1,0:T(8,128)(2,1)S(1)} async-done(((bf16[640,16,128]{2,1,0:T(8,128)(2,1)}), bf16[640,16,128]{2,1,0:T(8,128)(2,1)S(1)}, u32[]{:S(2)}, u32[]{:S(2)}) %all-to-all-start.1) | async-done | bytes 2621472 | tf_op jit(solution)/shard_map/all_to_all | solution.py:182
  239.3 1.8 combine.1
  241.1 0.9 copy.41
  (22 shorter events, 0.3 us)
Async XLA Ops:
  13.8 15.7 %copy-start.1 = (bf16[1,2048,384]{2,1,0:T(8,128)(2,1)S(1)}, bf16[1,2048,384]{2,1,0:T(8,128)(2,1)}, u32[]{:S(2)}) copy-start(bf16[1,2048,384]{2,1,0:T(8,128)(2,1)} %param.11) | copy-start | bytes 4718596
  13.8 15.8 %copy-start.2 = (bf16[1,2048,384]{2,1,0:T(8,128)(2,1)S(1)}, bf16[1,2048,384]{2,1,0:T(8,128)(2,1)}, u32[]{:S(2)}) copy-start(bf16[1,2048,384]{2,1,0:T(8,128)(2,1)} %param.12) | copy-start | bytes 4718596
  13.8 134.1 %all-to-all-start = ((bf16[1280,16,128]{2,1,0:T(8,128)(2,1)}), bf16[1280,16,128]{2,1,0:T(8,128)(2,1)}, u32[]{:S(2)}, u32[]{:S(2)}) async-start(bf16[1280,16,128]{2,1,0:T(8,128)(2,1)} %get-tuple-element.11), calls=%async_computation | async-start | bytes 10485760 | tf_op jit(solution)/shard_map/all_to_all | solution.py:182
  29.5 3.5 %collective-permute-start = (bf16[2048,384]{1,0:T(8,128)(2,1)S(1)}, bf16[2048,384]{1,0:T(8,128)(2,1)S(1)}, u32[]{:S(2)}, u32[]{:S(2)}) collective-permute-start(bf16[2048,384]{1,0:T(8,128)(2,1)S(1)} %bitcast.59), channel_id=1, source_target_pairs={{0,128},{128,0},{1,129},{129,1},{2,130},{130,2},{3,131},{131,3},{4... | collective-permute-start | bytes 4718600 | tf_op jit(solution)/shard_map/ppermute | solution.py:181
  29.6 7.9 %collective-permute-start.1 = (bf16[2048,384]{1,0:T(8,128)(2,1)S(1)}, bf16[2048,384]{1,0:T(8,128)(2,1)S(1)}, u32[]{:S(2)}, u32[]{:S(2)}) collective-permute-start(bf16[2048,384]{1,0:T(8,128)(2,1)S(1)} %bitcast.61), channel_id=1, source_target_pairs={{0,128},{128,0},{1,129},{129,1},{2,130},{130,2},{3,131},{131,3},{4... | collective-permute-start | bytes 4718600 | tf_op jit(solution)/shard_map/ppermute | solution.py:181
  30.1 8.5 %collective-permute-start.2 = (bf16[384,2048]{1,0:T(8,128)(2,1)}, bf16[384,2048]{1,0:T(8,128)(2,1)}, u32[]{:S(2)}, u32[]{:S(2)}) collective-permute-start(bf16[384,2048]{1,0:T(8,128)(2,1)} %bitcast.62), channel_id=1, source_target_pairs={{0,128},{128,0},{1,129},{129,1},{2,130},{130,2},{3,131},{131,3},{4... | collective-permute-start | bytes 4718600 | tf_op jit(solution)/shard_map/ppermute | solution.py:181
  33.0 4.5 %copy-start.3 = (bf16[2048,384]{1,0:T(8,128)(2,1)}, bf16[2048,384]{1,0:T(8,128)(2,1)S(1)}, u32[]{:S(2)}) copy-start(bf16[2048,384]{1,0:T(8,128)(2,1)S(1)} %collective-permute-done.gate_b) | copy-start | bytes 4718596
  37.5 1.1 copy-start.4
  166.5 72.8 %all-to-all-start.1 = ((bf16[640,16,128]{2,1,0:T(8,128)(2,1)}), bf16[640,16,128]{2,1,0:T(8,128)(2,1)S(1)}, u32[]{:S(2)}, u32[]{:S(2)}) async-start(bf16[640,16,128]{2,1,0:T(8,128)(2,1)} %get-tuple-element.12), calls=%async_computation.1 | async-start | bytes 5242880 | tf_op jit(solution)/shard_map/all_to_all | solution.py:182
  175.0 3.6 %copy-start.5 = (bf16[640,768]{1,0:T(8,128)(2,1)S(1)}, bf16[640,768]{1,0:T(8,128)(2,1)}, u32[]{:S(2)}) copy-start(bf16[640,768]{1,0:T(8,128)(2,1)} %get-tuple-element.15) | copy-start | bytes 2949124
  178.6 1.6 copy-start.7
  180.1 4.7 %collective-permute-start.5 = (bf16[384,2048]{1,0:T(8,128)(2,1)S(1)}, bf16[384,2048]{1,0:T(8,128)(2,1)S(1)}, u32[]{:S(2)}, u32[]{:S(2)}) collective-permute-start(bf16[384,2048]{1,0:T(8,128)(2,1)S(1)} %convolution_convert_fusion), channel_id=1, source_target_pairs={{0,128},{128,0},{1,129},{129,1},{2,130},{130,2},{3,131},{131,3},{4... | collective-permute-start | bytes 4718600 | tf_op jit(solution)/shard_map/ppermute | solution.py:181
  180.2 2.4 copy-start.6
  182.0 5.4 %collective-permute-start.3 = (bf16[2048,384]{1,0:T(8,128)(2,1)S(1)}, bf16[2048,384]{1,0:T(8,128)(2,1)S(1)}, u32[]{:S(2)}, u32[]{:S(2)}) collective-permute-start(bf16[2048,384]{1,0:T(8,128)(2,1)S(1)} %convolution_convert_fusion.2), channel_id=1, source_target_pairs={{0,128},{128,0},{1,129},{129,1},{2,130},{130,2},{3,131},{131,3},{4... | collective-permute-start | bytes 4718600 | tf_op jit(solution)/shard_map/ppermute | solution.py:181
  184.4 6.0 %collective-permute-start.4 = (bf16[2048,384]{1,0:T(8,128)(2,1)S(1)}, bf16[2048,384]{1,0:T(8,128)(2,1)S(1)}, u32[]{:S(2)}, u32[]{:S(2)}) collective-permute-start(bf16[2048,384]{1,0:T(8,128)(2,1)S(1)} %convolution_convert_fusion.1), channel_id=1, source_target_pairs={{0,128},{128,0},{1,129},{129,1},{2,130},{130,2},{3,131},{131,3},{4... | collective-permute-start | bytes 4718600 | tf_op jit(solution)/shard_map/ppermute | solution.py:181
  190.4 48.9 %copy-start = (s32[4,128]{1,0:T(4,128)S(1)}, s32[4,128]{1,0:T(4,128)}, u32[]{:S(2)}) copy-start(s32[4,128]{1,0:T(4,128)} %get-tuple-element.10.place) | copy-start | bytes 6148

commit v4 on v3

--- a/solution.py
+++ b/solution.py
@@ -13,46 +13,77 @@
 SMEM = pl.BlockSpec(memory_space=pltpu.SMEM)
 
 
-def fill_kernel(ids, gates, x, dy, out, place, send, count, sem):
+def fill_kernel(chunks, ids, gates, x, dy, out, place, v_x, v_dy, send, v_token, v_gate, token_of, gate_of, sems):
     top, tokens = ids.shape
-
-    def clear_count(e, carry):
-        count[e] = 0
+    blocks, lanes = send.shape[1:]
+    experts = send.shape[0] // (2 * CAP)
+    f32, bf16 = jnp.float32, jnp.bfloat16
+    expert_id = lax.broadcasted_iota(jnp.int32, (experts, tokens), 0)
+    names = [expert_id == ids[k : k + 1, :] for k in range(top)]
+    named = jnp.zeros((experts, tokens), f32)
+    gate = jnp.zeros((experts, tokens), f32)
+    for k in range(top):
+        named = named + names[k].astype(f32)
+        gate = gate + jnp.where(names[k], gates[k : k + 1, :].astype(f32), 0.0)
+    before = lax.broadcasted_iota(jnp.int32, (tokens, tokens), 0) < lax.broadcasted_iota(jnp.int32, (tokens, tokens), 1)
+    earlier = contract(named.astype(bf16), before.astype(f32).astype(bf16), ((1,), (0,)))
+    for k in range(top):
+        slot = jnp.sum(jnp.where(names[k], earlier, 0.0), axis=0, keepdims=True)
+        place[k : k + 1, :] = ids[k : k + 1, :] * CAP + slot.astype(jnp.int32)
+    number = lax.broadcasted_iota(jnp.int32, (8, tokens), 1).astype(f32).astype(bf16)
+    ones = jnp.ones((8, tokens), bf16)
+    last = ((1,), (1,))
+    for c in range(CAP):
+        holds = jnp.where(earlier == c, named, 0.0)
+        full = contract(ones, holds.astype(bf16), last)[:1]
+        token = contract(number, holds.astype(bf16), last)[:1]
+        v_token[c : c + 1, :] = jnp.where(full > 0.5, token, float(tokens)).astype(jnp.int32)
+        v_gate[c : c + 1, :] = contract(ones, (holds * gate).astype(bf16), last)[:1]
+    tables = [
+        pltpu.make_async_copy(v_token, token_of, sems.at[0]),
+        pltpu.make_async_copy(v_gate, gate_of, sems.at[1]),
+    ]
+    for t in tables:
+        t.start()
+    for rows, v in ((x, v_x), (dy, v_dy)):
+        v[pl.ds(0, tokens)] = rows[...].reshape(tokens, blocks, lanes)
+        v[tokens] = jnp.zeros((blocks, lanes), bf16)
+    for t in tables:
+        t.wait()
+
+    def one_expert(e, carry):
+        for c in range(CAP):
+            token, slot = token_of[c, e], e * (2 * CAP) + c
+            send[slot] = v_x[token]
+            send[slot + CAP] = (v_dy[token].astype(f32) * gate_of[c, e]).astype(bf16)
         return carry
 
-    lax.fori_loop(0, count.shape[0], clear_count, 0, unroll=8)
-    send[...] = jnp.zeros_like(send)
-
-    def one_token(t, carry):
-        x_row = x[t]
-        dy_row = dy[t].astype(jnp.float32)
-        for k in range(top):
-            expert = ids[k, t]
-            taken = count[expert]
-            count[expert] = taken + 1
-            place[k, t] = expert * CAP + taken
-            slot = expert * (2 * CAP) + taken
-            send[slot] = x_row
-            send[slot + CAP] = (dy_row * gates[k, t]).astype(jnp.bfloat16)
-        return carry
-
-    lax.fori_loop(0, tokens, one_token, 0, unroll=4)
-    done = pltpu.make_async_copy(send, out, sem)
-    done.start()
-    done.wait()
-
-
-def fill_slots(ids, gates, x, dy, experts):
-    shape = (experts * 2 * CAP,) + x.shape[1:]
+    some = experts // chunks
+    done = []
+    for i in range(chunks):
+        lax.fori_loop(i * some, (i + 1) * some, one_expert, 0, unroll=2)
+        r = pl.ds(i * some * 2 * CAP, some * 2 * CAP)
+        done.append(pltpu.make_async_copy(send.at[r], out.at[r], sems.at[2 + i]))
+        done[-1].start()
+    for d in done:
+        d.wait()
+
+
+def fill_slots(ids, gates, x, dy, experts, chunks=4):
+    tokens, width = x.shape
+    tile = (width // 128, 128)
+    shape = (experts * 2 * CAP,) + tile
+    vmem = lambda *shape: pltpu.VMEM(shape, x.dtype)
     return pl.pallas_call(
-        fill_kernel,
+        functools.partial(fill_kernel, chunks),
         out_shape=(jax.ShapeDtypeStruct(shape, x.dtype), jax.ShapeDtypeStruct(ids.shape, jnp.int32)),
-        in_specs=[SMEM, SMEM, VMEM, VMEM],
-        out_specs=(ANY, SMEM),
+        in_specs=[VMEM] * 4,
+        out_specs=(ANY, VMEM),
         scratch_shapes=[
-            pltpu.VMEM(shape, x.dtype),
-            pltpu.SMEM((experts,), jnp.int32),
-            pltpu.SemaphoreType.DMA,
+            vmem(tokens + 1, *tile), vmem(tokens + 1, *tile), vmem(*shape),
+            pltpu.VMEM((8, experts), jnp.int32), pltpu.VMEM((8, experts), jnp.float32),
+            pltpu.SMEM((8, experts), jnp.int32), pltpu.SMEM((8, experts), jnp.float32),
+            pltpu.SemaphoreType.DMA((2 + chunks,)),
         ],
         compiler_params=pltpu.CompilerParams(vmem_limit_bytes=58 * 2**20),
         name="fill_slots",
@@ -182,11 +213,7 @@
     exchange = lambda a: lax.all_to_all(a, "ep", split_axis=0, concat_axis=0, tiled=True)
 
     send, place = fill_slots(
-        expert_ids.T,
-        gate_values.T.astype(jnp.float32),
-        activations.reshape((tokens,) + lanes),
-        out_grad.reshape((tokens,) + lanes),
-        experts,
+        expert_ids.T, gate_values.T, activations, out_grad, experts
     )
     weights = []
     for w in (w_gate[0], w_up[0], w_down[0]):

time: 242 us -> 235 us (0.971)
  local copies, waits for them, and re-layouts: 9.54 us -> 5.65 us
    unnamed x19 -> x17, local copies, waits for them, and re-layouts: 6 us -> 2.11 us
where the time goes in v4:
time: 235 us
  waiting for transfers between devices  162 us (69%)
  Pallas kernels  26.5 us (11%)
  starting transfers between devices  25.9 us (11%)
  matrix products  13.7 us (6%)
  local copies, waits for them, and re-layouts  5.65 us (2%)
    all_to_all x2, waiting for transfers between devices, local(): lax.all_to_all(a, 'ep', split_axis=0, concat_axis=0, tiled=True)  155 us
    all_to_all x2, starting transfers between devices, local(): lax.all_to_all(a, 'ep', split_axis=0, concat_axis=0, tiled=True)  24.2 us
    pallas_call x1, Pallas kernels, row_grads(): pl.pallas_call(functools.partial(row_grads_kernel, parts, columns), out_s...  18.6 us
    dot_general x6, matrix products, contract(): lax.dot_general(left, right, (dims, ((), ())), preferred_element_type=jnp...  13.7 us
    ppermute x6, waiting for transfers between devices, local(): swap = lambda a: lax.ppermute(a, 'grp', [(0, 1), (1, 0)])  7.3 us
    pallas_call x1, Pallas kernels, fill_slots(): pl.pallas_call(functools.partial(fill_kernel, chunks), out_shape=(jax.Sha...  6.07 us
  transfers between devices with their start and end apart: 8, of which 4 were waited for; matrix products, arithmetic and copies ran while one was open for 7% of the time, Pallas kernels for 0%

profile of v4, /device:TPU:32, one launch (start us, length us, event | category | flops | bytes accessed | tf_op | source)
XLA Modules:
  0.0 234.9 jit_solution(7016197202163093604)
XLA Ops:
  0.6 6.1 %fill_slots.1 = (bf16[1280,16,128]{2,1,0:T(8,128)(2,1)}, s32[4,128]{1,0:T(4,128)}) custom-call(s32[4,128]{1,0:T(4,128)} %bitcast.48, bf16[4,128]{1,0:T(4,128)(2,1)} %bitcast.49, bf16[128,2048]{1,0:T(8,128)(2,1)} %x.1, bf16[128,2048]{1,0:T(8,128)(2,1)} %dy.1), custom_call_target="tpu_custom_call" | custom-call | tf_op jit(solution)/shard_map/fill_slots/pallas_call | solution.py:77
  6.7 15.7 %all-to-all-start = ((bf16[1280,16,128]{2,1,0:T(8,128)(2,1)}), bf16[1280,16,128]{2,1,0:T(8,128)(2,1)}, u32[]{:S(2)}, u32[]{:S(2)}) async-start(bf16[1280,16,128]{2,1,0:T(8,128)(2,1)} %get-tuple-element.11), calls=%async_computation | async-start | bytes 10485760 | tf_op jit(solution)/shard_map/all_to_all | solution.py:213
  22.4 0.1 collective-permute-start
  22.6 0.5 collective-permute-start.1
  23.0 0.1 collective-permute-start.2
  23.2 2.8 %collective-permute-done.gate_b = bf16[2048,384]{1,0:T(8,128)(2,1)S(1)} collective-permute-done((bf16[2048,384]{1,0:T(8,128)(2,1)S(1)}, bf16[2048,384]{1,0:T(8,128)(2,1)S(1)}, u32[]{:S(2)}, u32[]{:S(2)}) %collective-permute-start) | collective-permute-done | bytes 1572896 | tf_op jit(solution)/shard_map/ppermute | solution.py:212
  25.9 4.5 %collective-permute-done.1.up_b = bf16[2048,384]{1,0:T(8,128)(2,1)S(1)} collective-permute-done((bf16[2048,384]{1,0:T(8,128)(2,1)S(1)}, bf16[2048,384]{1,0:T(8,128)(2,1)S(1)}, u32[]{:S(2)}, u32[]{:S(2)}) %collective-permute-start.1) | collective-permute-done | bytes 1572896 | tf_op jit(solution)/shard_map/ppermute | solution.py:212
  30.4 1.1 copy-done.4
  31.6 109.2 %all-to-all-done = bf16[1280,16,128]{2,1,0:T(8,128)(2,1)} async-done(((bf16[1280,16,128]{2,1,0:T(8,128)(2,1)}), bf16[1280,16,128]{2,1,0:T(8,128)(2,1)}, u32[]{:S(2)}, u32[]{:S(2)}) %all-to-all-start) | async-done | bytes 5242912 | tf_op jit(solution)/shard_map/all_to_all | solution.py:213
  140.8 18.6 %row_grads.1 = (bf16[640,16,128]{2,1,0:T(8,128)(2,1)}, bf16[640,768]{1,0:T(8,128)(2,1)}, bf16[640,768]{1,0:T(8,128)(2,1)}, bf16[640,768]{1,0:T(8,128)(2,1)}) custom-call(bf16[128,10,16,128]{3,2,1,0:T(8,128)(2,1)} %bitcast.2.arrived, bf16[2048,384]{1,0:T(8,128)(2,1)} %bitcast.50, bf16[2048,384]{1,0:T(8,128)(2,1)} %copy-done.3, bf16[2048,384]{1,0:T(8,128)(2,1)} %bitcast.52, ...), custom_call_target="tpu_custom_call" | custom-call | flops 10066329600 | bytes 25165824 | tf_op jit(solution)/shard_map/row_grads/pallas_call | solution.py:163
  159.4 8.5 %all-to-all-start.1 = ((bf16[640,16,128]{2,1,0:T(8,128)(2,1)}), bf16[640,16,128]{2,1,0:T(8,128)(2,1)S(1)}, u32[]{:S(2)}, u32[]{:S(2)}) async-start(bf16[640,16,128]{2,1,0:T(8,128)(2,1)} %get-tuple-element.12), calls=%async_computation.1 | async-start | bytes 5242880 | tf_op jit(solution)/shard_map/all_to_all | solution.py:213
  168.0 3.5 %fusion.27 = (bf16[128,5,16,128]{3,2,1,0:T(8,128)(2,1)S(1)}, bf16[128,5,16,128]{3,2,1,0:T(8,128)(2,1)S(1)}) fusion(bf16[128,10,16,128]{3,2,1,0:T(8,128)(2,1)} %bitcast.2.arrived), kind=kLoop, calls=%fused_computation.28 | loop fusion | bytes 10485760 | tf_op jit(solution)/shard_map/slice | solution.py:226
  171.5 1.4 convolution_convert_fusion
  173.0 0.1 collective-permute-start.5
  173.1 1.8 convolution_convert_fusion.2
  174.9 0.6 collective-permute-start.3
  175.5 1.8 convolution_convert_fusion.1
  177.3 0.4 collective-permute-start.4
  177.7 2.6 %fusion.12 = bf16[1,384,2048]{2,1,0:T(8,128)(2,1)} fusion(bf16[384,2048]{1,0:T(8,128)(2,1)S(1)} %collective-permute-done.5, bf16[80,8,16,128]{3,2,1,0:T(8,128)(2,1)S(1)} %bitcast.46, bf16[640,768]{1,0:T(8,128)(2,1)S(1)} %copy-done.5), kind=kOutput, calls=%fused_computation.14 | convolution fusion | flops 1008992256 | bytes 6258688 | tf_op jit(solution)/shard_map/dot_general | solution.py:205
  180.3 3.0 %fusion.6 = bf16[1,2048,384]{2,1,0:T(8,128)(2,1)} fusion(bf16[2048,384]{1,0:T(8,128)(2,1)S(1)} %collective-permute-done.3, bf16[80,8,16,128]{3,2,1,0:T(8,128)(2,1)S(1)} %bitcast.43, bf16[640,768]{1,0:T(8,128)(2,1)S(1)} %copy-done.7), kind=kOutput, calls=%fused_computation.12 | convolution fusion | flops 1008992256 | bytes 6258688 | tf_op jit(solution)/shard_map/dot_general | solution.py:205
  183.3 3.0 %fusion.9 = bf16[1,2048,384]{2,1,0:T(8,128)(2,1)} fusion(bf16[2048,384]{1,0:T(8,128)(2,1)S(1)} %collective-permute-done.4, bf16[80,8,16,128]{3,2,1,0:T(8,128)(2,1)S(1)} %bitcast.44, bf16[640,768]{1,0:T(8,128)(2,1)S(1)} %copy-done.6), kind=kOutput, calls=%fused_computation.13 | convolution fusion | flops 1008992256 | bytes 6258688 | tf_op jit(solution)/shard_map/dot_general | solution.py:205
  186.4 45.9 %all-to-all-done.1.rows = bf16[640,16,128]{2,1,0:T(8,128)(2,1)S(1)} async-done(((bf16[640,16,128]{2,1,0:T(8,128)(2,1)}), bf16[640,16,128]{2,1,0:T(8,128)(2,1)S(1)}, u32[]{:S(2)}, u32[]{:S(2)}) %all-to-all-start.1) | async-done | bytes 2621472 | tf_op jit(solution)/shard_map/all_to_all | solution.py:213
  232.2 1.8 combine.1
  234.0 0.9 copy.39
  (19 shorter events, 0.0 us)
Async XLA Ops:
  6.7 15.7 %copy-start.1 = (bf16[1,2048,384]{2,1,0:T(8,128)(2,1)S(1)}, bf16[1,2048,384]{2,1,0:T(8,128)(2,1)}, u32[]{:S(2)}) copy-start(bf16[1,2048,384]{2,1,0:T(8,128)(2,1)} %param.11) | copy-start | bytes 4718596
  6.7 15.8 %copy-start.2 = (bf16[1,2048,384]{2,1,0:T(8,128)(2,1)S(1)}, bf16[1,2048,384]{2,1,0:T(8,128)(2,1)}, u32[]{:S(2)}) copy-start(bf16[1,2048,384]{2,1,0:T(8,128)(2,1)} %param.12) | copy-start | bytes 4718596
  6.7 134.1 %all-to-all-start = ((bf16[1280,16,128]{2,1,0:T(8,128)(2,1)}), bf16[1280,16,128]{2,1,0:T(8,128)(2,1)}, u32[]{:S(2)}, u32[]{:S(2)}) async-start(bf16[1280,16,128]{2,1,0:T(8,128)(2,1)} %get-tuple-element.11), calls=%async_computation | async-start | bytes 10485760 | tf_op jit(solution)/shard_map/all_to_all | solution.py:213
  22.4 3.5 %collective-permute-start = (bf16[2048,384]{1,0:T(8,128)(2,1)S(1)}, bf16[2048,384]{1,0:T(8,128)(2,1)S(1)}, u32[]{:S(2)}, u32[]{:S(2)}) collective-permute-start(bf16[2048,384]{1,0:T(8,128)(2,1)S(1)} %bitcast.51), channel_id=1, source_target_pairs={{0,128},{128,0},{1,129},{129,1},{2,130},{130,2},{3,131},{131,3},{4... | collective-permute-start | bytes 4718600 | tf_op jit(solution)/shard_map/ppermute | solution.py:212
  22.6 7.9 %collective-permute-start.1 = (bf16[2048,384]{1,0:T(8,128)(2,1)S(1)}, bf16[2048,384]{1,0:T(8,128)(2,1)S(1)}, u32[]{:S(2)}, u32[]{:S(2)}) collective-permute-start(bf16[2048,384]{1,0:T(8,128)(2,1)S(1)} %bitcast.53), channel_id=1, source_target_pairs={{0,128},{128,0},{1,129},{129,1},{2,130},{130,2},{3,131},{131,3},{4... | collective-permute-start | bytes 4718600 | tf_op jit(solution)/shard_map/ppermute | solution.py:212
  23.0 8.5 %collective-permute-start.2 = (bf16[384,2048]{1,0:T(8,128)(2,1)}, bf16[384,2048]{1,0:T(8,128)(2,1)}, u32[]{:S(2)}, u32[]{:S(2)}) collective-permute-start(bf16[384,2048]{1,0:T(8,128)(2,1)} %bitcast.54), channel_id=1, source_target_pairs={{0,128},{128,0},{1,129},{129,1},{2,130},{130,2},{3,131},{131,3},{4... | collective-permute-start | bytes 4718600 | tf_op jit(solution)/shard_map/ppermute | solution.py:212
  25.9 4.5 %copy-start.3 = (bf16[2048,384]{1,0:T(8,128)(2,1)}, bf16[2048,384]{1,0:T(8,128)(2,1)S(1)}, u32[]{:S(2)}) copy-start(bf16[2048,384]{1,0:T(8,128)(2,1)S(1)} %collective-permute-done.gate_b) | copy-start | bytes 4718596
  30.4 1.1 copy-start.4
  159.4 72.8 %all-to-all-start.1 = ((bf16[640,16,128]{2,1,0:T(8,128)(2,1)}), bf16[640,16,128]{2,1,0:T(8,128)(2,1)S(1)}, u32[]{:S(2)}, u32[]{:S(2)}) async-start(bf16[640,16,128]{2,1,0:T(8,128)(2,1)} %get-tuple-element.12), calls=%async_computation.1 | async-start | bytes 5242880 | tf_op jit(solution)/shard_map/all_to_all | solution.py:213
  168.0 3.6 %copy-start.5 = (bf16[640,768]{1,0:T(8,128)(2,1)S(1)}, bf16[640,768]{1,0:T(8,128)(2,1)}, u32[]{:S(2)}) copy-start(bf16[640,768]{1,0:T(8,128)(2,1)} %get-tuple-element.15) | copy-start | bytes 2949124
  171.5 1.6 copy-start.7
  173.0 4.7 %collective-permute-start.5 = (bf16[384,2048]{1,0:T(8,128)(2,1)S(1)}, bf16[384,2048]{1,0:T(8,128)(2,1)S(1)}, u32[]{:S(2)}, u32[]{:S(2)}) collective-permute-start(bf16[384,2048]{1,0:T(8,128)(2,1)S(1)} %convolution_convert_fusion), channel_id=1, source_target_pairs={{0,128},{128,0},{1,129},{129,1},{2,130},{130,2},{3,131},{131,3},{4... | collective-permute-start | bytes 4718600 | tf_op jit(solution)/shard_map/ppermute | solution.py:212
  173.1 2.4 %copy-start.6 = (bf16[640,768]{1,0:T(8,128)(2,1)S(1)}, bf16[640,768]{1,0:T(8,128)(2,1)}, u32[]{:S(2)}) copy-start(bf16[640,768]{1,0:T(8,128)(2,1)} %get-tuple-element.14) | copy-start | bytes 2949124
  174.9 5.4 %collective-permute-start.3 = (bf16[2048,384]{1,0:T(8,128)(2,1)S(1)}, bf16[2048,384]{1,0:T(8,128)(2,1)S(1)}, u32[]{:S(2)}, u32[]{:S(2)}) collective-permute-start(bf16[2048,384]{1,0:T(8,128)(2,1)S(1)} %convolution_convert_fusion.2), channel_id=1, source_target_pairs={{0,128},{128,0},{1,129},{129,1},{2,130},{130,2},{3,131},{131,3},{4... | collective-permute-start | bytes 4718600 | tf_op jit(solution)/shard_map/ppermute | solution.py:212
  177.3 6.1 %collective-permute-start.4 = (bf16[2048,384]{1,0:T(8,128)(2,1)S(1)}, bf16[2048,384]{1,0:T(8,128)(2,1)S(1)}, u32[]{:S(2)}, u32[]{:S(2)}) collective-permute-start(bf16[2048,384]{1,0:T(8,128)(2,1)S(1)} %convolution_convert_fusion.1), channel_id=1, source_target_pairs={{0,128},{128,0},{1,129},{129,1},{2,130},{130,2},{3,131},{131,3},{4... | collective-permute-start | bytes 4718600 | tf_op jit(solution)/shard_map/ppermute | solution.py:212
  183.3 48.9 %copy-start = (s32[4,128]{1,0:T(4,128)S(1)}, s32[4,128]{1,0:T(4,128)}, u32[]{:S(2)}) copy-start(s32[4,128]{1,0:T(4,128)} %get-tuple-element.10.place) | copy-start | bytes 6148

commit v5 on v4

--- a/solution.py
+++ b/solution.py
@@ -91,26 +91,21 @@
 
 
 def row_grads_kernel(
-    parts, columns, arrived, gate_a, gate_b, up_a, up_b, down_a, down_b,
-    out, weighted, grad_gate, grad_up,
-    v_x, v_dy, v_gate, v_up, v_down, v_out, v_weighted, v_grad_gate, v_grad_up,
-    x_sem, dy_sem, w_sem, out_sem,
+    parts, columns, arrived, w_gate, up, down, out, weighted, grad_gate, grad_up,
+    w_up, w_down, v_x, v_dy, v_out, v_weighted, v_grad_gate, v_grad_up, w_sem, x_sem, dy_sem, out_sem,
 ):
     sources, _, blocks, lanes = arrived.shape
-    half, width = down_a.shape
+    width = w_down.shape[1]
     some = sources // parts
     step, group = some * CAP, blocks // columns
     copy = pltpu.make_async_copy
-    sides = (pl.ds(0, half), pl.ds(half, half))
     x_in, dy_in = [], []
     for i in range(parts):
         s = pl.ds(i * some, some)
         x_in.append(copy(arrived.at[s, pl.ds(0, CAP)], v_x.at[s], x_sem.at[i]))
         dy_in.append(copy(arrived.at[s, pl.ds(CAP, CAP)], v_dy.at[s], dy_sem.at[i]))
-    gate_in = [copy(w, v_gate.at[:, d], w_sem.at[0 + j]) for j, (w, d) in enumerate(zip((gate_a, gate_b), sides))]
-    up_in = [copy(w, v_up.at[:, d], w_sem.at[2 + j]) for j, (w, d) in enumerate(zip((up_a, up_b), sides))]
-    down_in = [copy(w, v_down.at[d], w_sem.at[4 + j]) for j, (w, d) in enumerate(zip((down_a, down_b), sides))]
-    for c in [x_in[0], *gate_in, *up_in, dy_in[0], *down_in]:
+    up_in, down_in = copy(up, w_up, w_sem.at[0]), copy(down, w_down, w_sem.at[1])
+    for c in (x_in[0], up_in, dy_in[0], down_in):
         c.start()
     for i in range(1, parts):
         x_in[i].start()
@@ -121,29 +116,24 @@
         s, r = pl.ds(i * some, some), pl.ds(i * step, step)
         x_in[i].wait()
         x = v_x[s].reshape(step, width)
+        pre_gate = contract(x, w_gate[...], ((1,), (0,)))
         if i == 0:
-            for c in gate_in:
-                c.wait()
-        pre_gate = contract(x, v_gate[...], ((1,), (0,)))
-        if i == 0:
-            for c in up_in:
-                c.wait()
-        pre_up = contract(x, v_up[...], ((1,), (0,)))
+            up_in.wait()
+        pre_up = contract(x, w_up[...], ((1,), (0,)))
         sig = jax.nn.sigmoid(pre_gate)
         silu = pre_gate * sig
         v_weighted[r, :] = (silu * pre_up).astype(jnp.bfloat16)
         dy_in[i].wait()
         if i == 0:
-            for c in down_in:
-                c.wait()
-        grad_hidden = contract(v_dy[s].reshape(step, width), v_down[...], ((1,), (1,)))
+            down_in.wait()
+        grad_hidden = contract(v_dy[s].reshape(step, width), w_down[...], ((1,), (1,)))
         slope = pre_up * sig * (1.0 + pre_gate * (1.0 - sig))
         v_grad_gate[r, :] = (grad_hidden * slope).astype(jnp.bfloat16)
         v_grad_up[r, :] = (grad_hidden * silu).astype(jnp.bfloat16)
         for c in range(columns):
             w = pl.ds(c * group * lanes, group * lanes)
-            total = contract(v_grad_gate[r, :], v_gate[w, :], ((1,), (1,)))
-            total = total + contract(v_grad_up[r, :], v_up[w, :], ((1,), (1,)))
+            total = contract(v_grad_gate[r, :], w_gate[w, :], ((1,), (1,)))
+            total = total + contract(v_grad_up[r, :], w_up[w, :], ((1,), (1,)))
             v_out[r, pl.ds(c * group, group), :] = total.astype(jnp.bfloat16).reshape(step, group, lanes)
         pairs = ((v_out, out), (v_weighted, weighted), (v_grad_gate, grad_gate), (v_grad_up, grad_up))
         for j, (v, o) in enumerate(pairs):
@@ -153,49 +143,54 @@
         c.wait()
 
 
-def row_grads(arrived, gate_a, gate_b, up_a, up_b, down_a, down_b, parts=2, columns=2):
+def row_grads(arrived, w_gate, w_up, w_down, parts=2, columns=2):
     sources, _, blocks, lanes = arrived.shape
-    half, width = down_a.shape
-    rows, hidden = sources * CAP, 2 * half
-    struct = lambda *shape: jax.ShapeDtypeStruct(shape, jnp.bfloat16)
+    hidden, width = w_down.shape
+    rows = sources * CAP
+    struct = lambda *shape: pltpu.HBM(shape, jnp.bfloat16)
     vmem = lambda *shape: pltpu.VMEM(shape, jnp.bfloat16)
     dma = lambda n: pltpu.SemaphoreType.DMA((n,))
     return pl.pallas_call(
         functools.partial(row_grads_kernel, parts, columns),
         out_shape=(struct(rows, blocks, lanes),) + (struct(rows, hidden),) * 3,
-        in_specs=[ANY] * 7,
+        in_specs=[ANY, VMEM, ANY, ANY],
         out_specs=(ANY,) * 4,
         scratch_shapes=[
+            vmem(width, hidden), vmem(hidden, width),
             vmem(sources, CAP, blocks, lanes), vmem(sources, CAP, blocks, lanes),
-            vmem(width, hidden), vmem(width, hidden), vmem(hidden, width),
             vmem(rows, blocks, lanes), vmem(rows, hidden), vmem(rows, hidden), vmem(rows, hidden),
-            dma(parts), dma(parts), dma(6), dma(4 * parts),
+            dma(2), dma(parts), dma(parts), dma(4 * parts),
         ],
-        compiler_params=pltpu.CompilerParams(vmem_limit_bytes=58 * 2**20),
+        compiler_params=pltpu.CompilerParams(vmem_limit_bytes=40 * 2**20),
         cost_estimate=pl.CostEstimate(
             flops=10 * rows * hidden * width, bytes_accessed=24 * 2**20, transcendentals=rows * hidden
         ),
         name="row_grads",
-    )(arrived, gate_a, gate_b, up_a, up_b, down_a, down_b)
-
-
-def combine_kernel(place, rows, out):
+    )(arrived, *(
+        pltpu.with_memory_space_constraint(w, space)
+        for w, space in ((w_gate, pltpu.VMEM), (w_up, pltpu.HBM), (w_down, pltpu.HBM))
+    ))
+
+
+def combine_kernel(place, rows, out, sums):
     def one_token(t, carry):
         total = rows[place[0, t]].astype(jnp.float32)
         for k in range(1, place.shape[0]):
             total = total + rows[place[k, t]].astype(jnp.float32)
-        out[t] = total.astype(jnp.bfloat16)
+        sums[t] = total.astype(jnp.bfloat16)
         return carry
 
-    lax.fori_loop(0, out.shape[0], one_token, 0, unroll=2)
-
-
-def combine(place, rows, tokens):
+    lax.fori_loop(0, out.shape[0], one_token, 0, unroll=4)
+    out[...] = sums[...].reshape(out.shape)
+
+
+def combine(place, rows, tokens, width):
     return pl.pallas_call(
         combine_kernel,
-        out_shape=jax.ShapeDtypeStruct((tokens,) + rows.shape[1:], jnp.bfloat16),
+        out_shape=jax.ShapeDtypeStruct((tokens, width), jnp.bfloat16),
         in_specs=[SMEM, VMEM],
         out_specs=VMEM,
+        scratch_shapes=[pltpu.VMEM((tokens,) + rows.shape[1:], jnp.bfloat16)],
         compiler_params=pltpu.CompilerParams(vmem_limit_bytes=16 * 2**20),
         name="combine",
     )(place, rows)
@@ -215,9 +210,10 @@
     send, place = fill_slots(
         expert_ids.T, gate_values.T, activations, out_grad, experts
     )
-    weights = []
-    for w in (w_gate[0], w_up[0], w_down[0]):
-        weights += [w, swap(w)]
+    weights = [
+        jnp.concatenate([w[0], swap(w[0])], axis=axis)
+        for w, axis in ((w_gate, 1), (w_up, 1), (w_down, 0))
+    ]
     arrived = exchange(send).reshape((experts, 2 * CAP) + lanes)
     row_grad, weighted, grad_pre_gate, grad_pre_up = row_grads(arrived, *weights)
     returned = exchange(row_grad)
@@ -238,7 +234,7 @@
         contract(weighted[:, :half], dy, rows_t),
     )
     grads = [(m + t.astype(jnp.float32)).astype(jnp.bfloat16)[None] for m, t in zip(mine, theirs)]
-    grad_input = combine(place, returned, tokens).reshape(tokens, width)
+    grad_input = combine(place, returned, tokens, width)
     return (grad_input, *grads)
 
 

time: 235 us -> 232 us (0.987)
  other arithmetic: 0 us -> 8.49 us
  waiting for transfers between devices: 162 us -> 155 us
    concatenate x0 -> x3, other arithmetic: none -> 8.49 us  [local(): jnp.concatenate([w[0], swap(w[0])], axis=axis)]
    all_to_all x2, waiting for transfers between devices: 155 us -> 151 us  [local(): lax.all_to_all(a, 'ep', split_axis=0, concat_axis=0, tiled=True)]
    ppermute x6, waiting for transfers between devices: 7.3 us -> 4.05 us  [local(): swap = lambda a: lax.ppermute(a, 'grp', [(0, 1), (1, 0)])]
    pallas_call x1, Pallas kernels: 18.6 us -> 15.9 us  [row_grads(): pl.pallas_call(functools.partial(row_grads_kernel, parts, columns), out_s...]
  transfers between devices with their start and end apart: 8 -> 8, of which waited for: 4 -> 3; matrix products, arithmetic and copies ran while one was open for 7% -> 11% of each run, Pallas kernels for 0% -> 0%
where the time goes in v5:
time: 232 us
  waiting for transfers between devices  155 us (67%)
  starting transfers between devices  25.8 us (11%)
  Pallas kernels  24.5 us (11%)
  matrix products  13.7 us (6%)
  other arithmetic  8.49 us (4%)
  local copies, waits for them, and re-layouts  3.57 us (2%)
    all_to_all x2, waiting for transfers between devices, local(): lax.all_to_all(a, 'ep', split_axis=0, concat_axis=0, tiled=True)  151 us
    all_to_all x2, starting transfers between devices, local(): lax.all_to_all(a, 'ep', split_axis=0, concat_axis=0, tiled=True)  24.1 us
    pallas_call x1, Pallas kernels, row_grads(): pl.pallas_call(functools.partial(row_grads_kernel, parts, columns), out_s...  15.9 us
    dot_general x6, matrix products, contract(): lax.dot_general(left, right, (dims, ((), ())), preferred_element_type=jnp...  13.7 us
    concatenate x3, other arithmetic, local(): jnp.concatenate([w[0], swap(w[0])], axis=axis)  8.49 us
    pallas_call x1, Pallas kernels, fill_slots(): pl.pallas_call(functools.partial(fill_kernel, chunks), out_shape=(jax.Sha...  6.07 us
  transfers between devices with their start and end apart: 8, of which 3 were waited for; matrix products, arithmetic and copies ran while one was open for 11% of the time, Pallas kernels for 0%

profile of v5, /device:TPU:32, one launch (start us, length us, event | category | flops | bytes accessed | tf_op | source)
XLA Modules:
  0.0 231.8 jit_solution(1217074752814829415)
XLA Ops:
  0.6 6.1 %fill_slots.1 = (bf16[1280,16,128]{2,1,0:T(8,128)(2,1)}, s32[4,128]{1,0:T(4,128)}) custom-call(s32[4,128]{1,0:T(4,128)} %bitcast.50, bf16[4,128]{1,0:T(4,128)(2,1)} %bitcast.51, bf16[128,2048]{1,0:T(8,128)(2,1)} %x.1, bf16[128,2048]{1,0:T(8,128)(2,1)} %dy.1), custom_call_target="tpu_custom_call" | custom-call | tf_op jit(solution)/shard_map/fill_slots/pallas_call | solution.py:77
  6.7 15.6 %all-to-all-start = ((bf16[1280,16,128]{2,1,0:T(8,128)(2,1)}), bf16[1280,16,128]{2,1,0:T(8,128)(2,1)}, u32[]{:S(2)}, u32[]{:S(2)}) async-start(bf16[1280,16,128]{2,1,0:T(8,128)(2,1)} %get-tuple-element.11), calls=%async_computation | async-start | bytes 10485760 | tf_op jit(solution)/shard_map/all_to_all | solution.py:208
  22.3 0.1 collective-permute-start
  22.4 0.5 collective-permute-start.1
  22.9 0.1 collective-permute-start.2
  23.0 4.0 %collective-permute-done = bf16[2048,384]{1,0:T(8,128)(2,1)S(1)} collective-permute-done((bf16[2048,384]{1,0:T(8,128)(2,1)S(1)}, bf16[2048,384]{1,0:T(8,128)(2,1)S(1)}, u32[]{:S(2)}, u32[]{:S(2)}) %collective-permute-start) | collective-permute-done | bytes 1572896 | tf_op jit(solution)/shard_map/ppermute | solution.py:207
  27.0 1.7 pad_maximum_fusion.w_gate
  28.7 3.4 %pad_maximum_fusion.1.up = bf16[2048,768]{1,0:T(8,128)(2,1)} fusion(bf16[2048,384]{1,0:T(8,128)(2,1)S(1)} %collective-permute-done.1, bf16[2048,384]{1,0:T(8,128)(2,1)} %bitcast.4), kind=kLoop, calls=%fused_computation.1 | loop fusion | flops 6291456 | bytes 6291456 | tf_op jit(solution)/shard_map/concatenate | solution.py:214
  32.1 3.4 %pad_maximum_fusion.2.down = bf16[768,2048]{1,0:T(8,128)(2,1)} fusion(bf16[384,2048]{1,0:T(8,128)(2,1)S(1)} %collective-permute-done.2, bf16[384,2048]{1,0:T(8,128)(2,1)} %bitcast.5), kind=kLoop, calls=%fused_computation.2 | loop fusion | flops 6291456 | bytes 6291456 | tf_op jit(solution)/shard_map/concatenate | solution.py:214
  35.5 105.1 %all-to-all-done = bf16[1280,16,128]{2,1,0:T(8,128)(2,1)} async-done(((bf16[1280,16,128]{2,1,0:T(8,128)(2,1)}), bf16[1280,16,128]{2,1,0:T(8,128)(2,1)}, u32[]{:S(2)}, u32[]{:S(2)}) %all-to-all-start) | async-done | bytes 5242912 | tf_op jit(solution)/shard_map/all_to_all | solution.py:208
  140.7 15.9 %row_grads.1 = (bf16[640,16,128]{2,1,0:T(8,128)(2,1)}, bf16[640,768]{1,0:T(8,128)(2,1)}, bf16[640,768]{1,0:T(8,128)(2,1)}, bf16[640,768]{1,0:T(8,128)(2,1)}) custom-call(bf16[128,10,16,128]{3,2,1,0:T(8,128)(2,1)} %bitcast.2.arrived, bf16[2048,768]{1,0:T(8,128)(2,1)S(1)} %pad_maximum_fusion.w_gate, bf16[2048,768]{1,0:T(8,128)(2,1)} %pad_maximum_fusion.1.up, ...), custom_call_target="tpu_custom_call" | custom-call | flops 10066329600 | bytes 25165824 | tf_op jit(solution)/shard_map/row_grads/pallas_call | solution.py:153
  156.5 8.5 %all-to-all-start.1 = ((bf16[640,16,128]{2,1,0:T(8,128)(2,1)}), bf16[640,16,128]{2,1,0:T(8,128)(2,1)S(1)}, u32[]{:S(2)}, u32[]{:S(2)}) async-start(bf16[640,16,128]{2,1,0:T(8,128)(2,1)} %get-tuple-element.12), calls=%async_computation.1 | async-start | bytes 5242880 | tf_op jit(solution)/shard_map/all_to_all | solution.py:208
  165.1 3.5 %fusion.36 = (bf16[128,5,16,128]{3,2,1,0:T(8,128)(2,1)S(1)}, bf16[128,5,16,128]{3,2,1,0:T(8,128)(2,1)S(1)}) fusion(bf16[128,10,16,128]{3,2,1,0:T(8,128)(2,1)} %bitcast.2.arrived), kind=kLoop, calls=%fused_computation.33 | loop fusion | bytes 10485760 | tf_op jit(solution)/shard_map/slice | solution.py:222
  168.6 1.4 convolution_convert_fusion
  170.1 0.1 collective-permute-start.5
  170.2 1.8 convolution_convert_fusion.2
  172.0 0.6 collective-permute-start.3
  172.6 1.8 convolution_convert_fusion.1
  174.4 0.4 collective-permute-start.4
  174.8 2.6 %fusion.21 = bf16[1,384,2048]{2,1,0:T(8,128)(2,1)} fusion(bf16[384,2048]{1,0:T(8,128)(2,1)S(1)} %collective-permute-done.5, bf16[80,8,16,128]{3,2,1,0:T(8,128)(2,1)S(1)} %bitcast.47, bf16[640,768]{1,0:T(8,128)(2,1)S(1)} %copy-done.2), kind=kOutput, calls=%fused_computation.20 | convolution fusion | flops 1008992256 | bytes 6258688 | tf_op jit(solution)/shard_map/dot_general | solution.py:200
  177.4 3.0 %fusion.15 = bf16[1,2048,384]{2,1,0:T(8,128)(2,1)} fusion(bf16[2048,384]{1,0:T(8,128)(2,1)S(1)} %collective-permute-done.3, bf16[80,8,16,128]{3,2,1,0:T(8,128)(2,1)S(1)} %bitcast.44, bf16[640,768]{1,0:T(8,128)(2,1)S(1)} %copy-done.4), kind=kOutput, calls=%fused_computation.18 | convolution fusion | flops 1008992256 | bytes 6258688 | tf_op jit(solution)/shard_map/dot_general | solution.py:200
  180.4 3.0 %fusion.18 = bf16[1,2048,384]{2,1,0:T(8,128)(2,1)} fusion(bf16[2048,384]{1,0:T(8,128)(2,1)S(1)} %collective-permute-done.4, bf16[80,8,16,128]{3,2,1,0:T(8,128)(2,1)S(1)} %bitcast.45, bf16[640,768]{1,0:T(8,128)(2,1)S(1)} %copy-done.3), kind=kOutput, calls=%fused_computation.19 | convolution fusion | flops 1008992256 | bytes 6258688 | tf_op jit(solution)/shard_map/dot_general | solution.py:200
  183.4 45.9 %all-to-all-done.1.rows = bf16[640,16,128]{2,1,0:T(8,128)(2,1)S(1)} async-done(((bf16[640,16,128]{2,1,0:T(8,128)(2,1)}), bf16[640,16,128]{2,1,0:T(8,128)(2,1)S(1)}, u32[]{:S(2)}, u32[]{:S(2)}) %all-to-all-start.1) | async-done | bytes 2621472 | tf_op jit(solution)/shard_map/all_to_all | solution.py:208
  229.3 2.5 %combine.1 = bf16[128,2048]{1,0:T(8,128)(2,1)} custom-call(s32[4,128]{1,0:T(4,128)S(1)} %copy-done, bf16[640,16,128]{2,1,0:T(8,128)(2,1)S(1)} %all-to-all-done.1.rows), custom_call_target="tpu_custom_call" | custom-call | tf_op jit(solution)/shard_map/combine/pallas_call | solution.py:188
  (15 shorter events, 0.0 us)
Async XLA Ops:
  6.7 15.6 %copy-start.1 = (bf16[1,2048,384]{2,1,0:T(8,128)(2,1)S(1)}, bf16[1,2048,384]{2,1,0:T(8,128)(2,1)}, u32[]{:S(2)}) copy-start(bf16[1,2048,384]{2,1,0:T(8,128)(2,1)} %param.11) | copy-start | bytes 4718596
  6.7 133.9 %all-to-all-start = ((bf16[1280,16,128]{2,1,0:T(8,128)(2,1)}), bf16[1280,16,128]{2,1,0:T(8,128)(2,1)}, u32[]{:S(2)}, u32[]{:S(2)}) async-start(bf16[1280,16,128]{2,1,0:T(8,128)(2,1)} %get-tuple-element.11), calls=%async_computation | async-start | bytes 10485760 | tf_op jit(solution)/shard_map/all_to_all | solution.py:208
  22.3 4.7 %collective-permute-start = (bf16[2048,384]{1,0:T(8,128)(2,1)S(1)}, bf16[2048,384]{1,0:T(8,128)(2,1)S(1)}, u32[]{:S(2)}, u32[]{:S(2)}) collective-permute-start(bf16[2048,384]{1,0:T(8,128)(2,1)S(1)} %bitcast.49), channel_id=1, source_target_pairs={{0,128},{128,0},{1,129},{129,1},{2,130},{130,2},{3,131},{131,3},{4... | collective-permute-start | bytes 4718600 | tf_op jit(solution)/shard_map/ppermute | solution.py:207
  22.4 6.3 %collective-permute-start.1 = (bf16[2048,384]{1,0:T(8,128)(2,1)}, bf16[2048,384]{1,0:T(8,128)(2,1)S(1)}, u32[]{:S(2)}, u32[]{:S(2)}) collective-permute-start(bf16[2048,384]{1,0:T(8,128)(2,1)} %bitcast.4), channel_id=1, source_target_pairs={{0,128},{128,0},{1,129},{129,1},{2,130},{130,2},{3,131},{131,3},{4... | collective-permute-start | bytes 4718600 | tf_op jit(solution)/shard_map/ppermute | solution.py:207
  22.9 9.2 %collective-permute-start.2 = (bf16[384,2048]{1,0:T(8,128)(2,1)}, bf16[384,2048]{1,0:T(8,128)(2,1)S(1)}, u32[]{:S(2)}, u32[]{:S(2)}) collective-permute-start(bf16[384,2048]{1,0:T(8,128)(2,1)} %bitcast.5), channel_id=1, source_target_pairs={{0,128},{128,0},{1,129},{129,1},{2,130},{130,2},{3,131},{131,3},{4... | collective-permute-start | bytes 4718600 | tf_op jit(solution)/shard_map/ppermute | solution.py:207
  156.5 72.8 %all-to-all-start.1 = ((bf16[640,16,128]{2,1,0:T(8,128)(2,1)}), bf16[640,16,128]{2,1,0:T(8,128)(2,1)S(1)}, u32[]{:S(2)}, u32[]{:S(2)}) async-start(bf16[640,16,128]{2,1,0:T(8,128)(2,1)} %get-tuple-element.12), calls=%async_computation.1 | async-start | bytes 5242880 | tf_op jit(solution)/shard_map/all_to_all | solution.py:208
  165.1 3.6 %copy-start.2 = (bf16[640,768]{1,0:T(8,128)(2,1)S(1)}, bf16[640,768]{1,0:T(8,128)(2,1)}, u32[]{:S(2)}) copy-start(bf16[640,768]{1,0:T(8,128)(2,1)} %get-tuple-element.15) | copy-start | bytes 2949124
  168.6 1.6 copy-start.4
  170.1 4.7 %collective-permute-start.5 = (bf16[384,2048]{1,0:T(8,128)(2,1)S(1)}, bf16[384,2048]{1,0:T(8,128)(2,1)S(1)}, u32[]{:S(2)}, u32[]{:S(2)}) collective-permute-start(bf16[384,2048]{1,0:T(8,128)(2,1)S(1)} %convolution_convert_fusion), channel_id=1, source_target_pairs={{0,128},{128,0},{1,129},{129,1},{2,130},{130,2},{3,131},{131,3},{4... | collective-permute-start | bytes 4718600 | tf_op jit(solution)/shard_map/ppermute | solution.py:207
  170.2 2.4 %copy-start.3 = (bf16[640,768]{1,0:T(8,128)(2,1)S(1)}, bf16[640,768]{1,0:T(8,128)(2,1)}, u32[]{:S(2)}) copy-start(bf16[640,768]{1,0:T(8,128)(2,1)} %get-tuple-element.14) | copy-start | bytes 2949124
  172.0 5.4 %collective-permute-start.3 = (bf16[2048,384]{1,0:T(8,128)(2,1)S(1)}, bf16[2048,384]{1,0:T(8,128)(2,1)S(1)}, u32[]{:S(2)}, u32[]{:S(2)}) collective-permute-start(bf16[2048,384]{1,0:T(8,128)(2,1)S(1)} %convolution_convert_fusion.2), channel_id=1, source_target_pairs={{0,128},{128,0},{1,129},{129,1},{2,130},{130,2},{3,131},{131,3},{4... | collective-permute-start | bytes 4718600 | tf_op jit(solution)/shard_map/ppermute | solution.py:207
  174.4 6.0 %collective-permute-start.4 = (bf16[2048,384]{1,0:T(8,128)(2,1)S(1)}, bf16[2048,384]{1,0:T(8,128)(2,1)S(1)}, u32[]{:S(2)}, u32[]{:S(2)}) collective-permute-start(bf16[2048,384]{1,0:T(8,128)(2,1)S(1)} %convolution_convert_fusion.1), channel_id=1, source_target_pairs={{0,128},{128,0},{1,129},{129,1},{2,130},{130,2},{3,131},{131,3},{4... | collective-permute-start | bytes 4718600 | tf_op jit(solution)/shard_map/ppermute | solution.py:207
  180.4 48.9 %copy-start = (s32[4,128]{1,0:T(4,128)S(1)}, s32[4,128]{1,0:T(4,128)}, u32[]{:S(2)}) copy-start(s32[4,128]{1,0:T(4,128)} %get-tuple-element.10.place) | copy-start | bytes 6148

commit v6 on v5

--- a/solution.py
+++ b/solution.py
@@ -13,9 +13,15 @@
 SMEM = pl.BlockSpec(memory_space=pltpu.SMEM)
 
 
-def fill_kernel(chunks, ids, gates, x, dy, out, place, v_x, v_dy, send, v_token, v_gate, token_of, gate_of, sems):
+def fill_kernel(chunks, ids, gates, x, dy, out, place, x_rows, dy_rows, v_x, v_dy, send, v_token, v_gate, token_of, gate_of, sems):
     top, tokens = ids.shape
     blocks, lanes = send.shape[1:]
+    loads = [
+        pltpu.make_async_copy(x, x_rows, sems.at[2 + chunks]),
+        pltpu.make_async_copy(dy, dy_rows, sems.at[3 + chunks]),
+    ]
+    for c in loads:
+        c.start()
     experts = send.shape[0] // (2 * CAP)
     f32, bf16 = jnp.float32, jnp.bfloat16
     expert_id = lax.broadcasted_iota(jnp.int32, (experts, tokens), 0)
@@ -45,7 +51,8 @@
     ]
     for t in tables:
         t.start()
-    for rows, v in ((x, v_x), (dy, v_dy)):
+    for rows, v, load in ((x_rows, v_x, loads[0]), (dy_rows, v_dy, loads[1])):
+        load.wait()
         v[pl.ds(0, tokens)] = rows[...].reshape(tokens, blocks, lanes)
         v[tokens] = jnp.zeros((blocks, lanes), bf16)
     for t in tables:
@@ -69,7 +76,7 @@
         d.wait()
 
 
-def fill_slots(ids, gates, x, dy, experts, chunks=4):
+def fill_slots(ids, gates, x, dy, experts, chunks=8):
     tokens, width = x.shape
     tile = (width // 128, 128)
     shape = (experts * 2 * CAP,) + tile
@@ -77,13 +84,14 @@
     return pl.pallas_call(
         functools.partial(fill_kernel, chunks),
         out_shape=(jax.ShapeDtypeStruct(shape, x.dtype), jax.ShapeDtypeStruct(ids.shape, jnp.int32)),
-        in_specs=[VMEM] * 4,
+        in_specs=[VMEM, VMEM, ANY, ANY],
         out_specs=(ANY, VMEM),
         scratch_shapes=[
+            vmem(tokens, width), vmem(tokens, width),
             vmem(tokens + 1, *tile), vmem(tokens + 1, *tile), vmem(*shape),
             pltpu.VMEM((8, experts), jnp.int32), pltpu.VMEM((8, experts), jnp.float32),
             pltpu.SMEM((8, experts), jnp.int32), pltpu.SMEM((8, experts), jnp.float32),
-            pltpu.SemaphoreType.DMA((2 + chunks,)),
+            pltpu.SemaphoreType.DMA((4 + chunks,)),
         ],
         compiler_params=pltpu.CompilerParams(vmem_limit_bytes=58 * 2**20),
         name="fill_slots",
@@ -180,7 +188,7 @@
         sums[t] = total.astype(jnp.bfloat16)
         return carry
 
-    lax.fori_loop(0, out.shape[0], one_token, 0, unroll=4)
+    lax.fori_loop(0, out.shape[0], one_token, 0, unroll=8)
     out[...] = sums[...].reshape(out.shape)
 
 

time: 232 us -> 231 us (level)
  no operation moved by 1% of the time
where the time goes in v6:
time: 231 us
  waiting for transfers between devices  155 us (67%)
  starting transfers between devices  25.8 us (11%)
  Pallas kernels  23.6 us (10%)
  matrix products  13.7 us (6%)
  other arithmetic  8.49 us (4%)
  local copies, waits for them, and re-layouts  3.57 us (2%)
    all_to_all x2, waiting for transfers between devices, local(): lax.all_to_all(a, 'ep', split_axis=0, concat_axis=0, tiled=True)  151 us
    all_to_all x2, starting transfers between devices, local(): lax.all_to_all(a, 'ep', split_axis=0, concat_axis=0, tiled=True)  24.1 us
    pallas_call x1, Pallas kernels, row_grads(): pl.pallas_call(functools.partial(row_grads_kernel, parts, columns), out_s...  15.9 us
    dot_general x6, matrix products, contract(): lax.dot_general(left, right, (dims, ((), ())), preferred_element_type=jnp...  13.7 us
    concatenate x3, other arithmetic, local(): jnp.concatenate([w[0], swap(w[0])], axis=axis)  8.49 us
    pallas_call x1, Pallas kernels, fill_slots(): pl.pallas_call(functools.partial(fill_kernel, chunks), out_shape=(jax.Sha...  5.31 us
  transfers between devices with their start and end apart: 8, of which 3 were waited for; matrix products, arithmetic and copies ran while one was open for 11% of the time, Pallas kernels for 0%

profile of v6, /device:TPU:32, one launch (start us, length us, event | category | flops | bytes accessed | tf_op | source)
XLA Modules:
  0.0 231.0 jit_solution(10362767592940982638)
XLA Ops:
  0.6 5.3 %fill_slots.1 = (bf16[1280,16,128]{2,1,0:T(8,128)(2,1)}, s32[4,128]{1,0:T(4,128)}) custom-call(s32[4,128]{1,0:T(4,128)} %bitcast.50, bf16[4,128]{1,0:T(4,128)(2,1)} %bitcast.51, bf16[128,2048]{1,0:T(8,128)(2,1)} %x.1, bf16[128,2048]{1,0:T(8,128)(2,1)} %dy.1), custom_call_target="tpu_custom_call" | custom-call | tf_op jit(solution)/shard_map/fill_slots/pallas_call | solution.py:84
  6.0 15.6 %all-to-all-start = ((bf16[1280,16,128]{2,1,0:T(8,128)(2,1)}), bf16[1280,16,128]{2,1,0:T(8,128)(2,1)}, u32[]{:S(2)}, u32[]{:S(2)}) async-start(bf16[1280,16,128]{2,1,0:T(8,128)(2,1)} %get-tuple-element.11), calls=%async_computation | async-start | bytes 10485760 | tf_op jit(solution)/shard_map/all_to_all | solution.py:216
  21.5 0.1 collective-permute-start
  21.6 0.5 collective-permute-start.1
  22.1 0.1 collective-permute-start.2
  22.2 4.0 %collective-permute-done = bf16[2048,384]{1,0:T(8,128)(2,1)S(1)} collective-permute-done((bf16[2048,384]{1,0:T(8,128)(2,1)S(1)}, bf16[2048,384]{1,0:T(8,128)(2,1)S(1)}, u32[]{:S(2)}, u32[]{:S(2)}) %collective-permute-start) | collective-permute-done | bytes 1572896 | tf_op jit(solution)/shard_map/ppermute | solution.py:215
  26.3 1.7 pad_maximum_fusion.w_gate
  27.9 3.4 %pad_maximum_fusion.1.up = bf16[2048,768]{1,0:T(8,128)(2,1)} fusion(bf16[2048,384]{1,0:T(8,128)(2,1)S(1)} %collective-permute-done.1, bf16[2048,384]{1,0:T(8,128)(2,1)} %bitcast.4), kind=kLoop, calls=%fused_computation.1 | loop fusion | flops 6291456 | bytes 6291456 | tf_op jit(solution)/shard_map/concatenate | solution.py:222
  31.4 3.4 %pad_maximum_fusion.2.down = bf16[768,2048]{1,0:T(8,128)(2,1)} fusion(bf16[384,2048]{1,0:T(8,128)(2,1)S(1)} %collective-permute-done.2, bf16[384,2048]{1,0:T(8,128)(2,1)} %bitcast.5), kind=kLoop, calls=%fused_computation.2 | loop fusion | flops 6291456 | bytes 6291456 | tf_op jit(solution)/shard_map/concatenate | solution.py:222
  34.8 105.1 %all-to-all-done = bf16[1280,16,128]{2,1,0:T(8,128)(2,1)} async-done(((bf16[1280,16,128]{2,1,0:T(8,128)(2,1)}), bf16[1280,16,128]{2,1,0:T(8,128)(2,1)}, u32[]{:S(2)}, u32[]{:S(2)}) %all-to-all-start) | async-done | bytes 5242912 | tf_op jit(solution)/shard_map/all_to_all | solution.py:216
  139.9 15.9 %row_grads.1 = (bf16[640,16,128]{2,1,0:T(8,128)(2,1)}, bf16[640,768]{1,0:T(8,128)(2,1)}, bf16[640,768]{1,0:T(8,128)(2,1)}, bf16[640,768]{1,0:T(8,128)(2,1)}) custom-call(bf16[128,10,16,128]{3,2,1,0:T(8,128)(2,1)} %bitcast.2.arrived, bf16[2048,768]{1,0:T(8,128)(2,1)S(1)} %pad_maximum_fusion.w_gate, bf16[2048,768]{1,0:T(8,128)(2,1)} %pad_maximum_fusion.1.up, ...), custom_call_target="tpu_custom_call" | custom-call | flops 10066329600 | bytes 25165824 | tf_op jit(solution)/shard_map/row_grads/pallas_call | solution.py:161
  155.8 8.5 %all-to-all-start.1 = ((bf16[640,16,128]{2,1,0:T(8,128)(2,1)}), bf16[640,16,128]{2,1,0:T(8,128)(2,1)S(1)}, u32[]{:S(2)}, u32[]{:S(2)}) async-start(bf16[640,16,128]{2,1,0:T(8,128)(2,1)} %get-tuple-element.12), calls=%async_computation.1 | async-start | bytes 5242880 | tf_op jit(solution)/shard_map/all_to_all | solution.py:216
  164.3 3.5 %fusion.36 = (bf16[128,5,16,128]{3,2,1,0:T(8,128)(2,1)S(1)}, bf16[128,5,16,128]{3,2,1,0:T(8,128)(2,1)S(1)}) fusion(bf16[128,10,16,128]{3,2,1,0:T(8,128)(2,1)} %bitcast.2.arrived), kind=kLoop, calls=%fused_computation.33 | loop fusion | bytes 10485760 | tf_op jit(solution)/shard_map/slice | solution.py:230
  167.9 1.4 convolution_convert_fusion
  169.3 0.1 collective-permute-start.5
  169.4 1.8 convolution_convert_fusion.2
  171.2 0.6 collective-permute-start.3
  171.8 1.8 convolution_convert_fusion.1
  173.6 0.4 collective-permute-start.4
  174.0 2.6 %fusion.21 = bf16[1,384,2048]{2,1,0:T(8,128)(2,1)} fusion(bf16[384,2048]{1,0:T(8,128)(2,1)S(1)} %collective-permute-done.5, bf16[80,8,16,128]{3,2,1,0:T(8,128)(2,1)S(1)} %bitcast.47, bf16[640,768]{1,0:T(8,128)(2,1)S(1)} %copy-done.2), kind=kOutput, calls=%fused_computation.20 | convolution fusion | flops 1008992256 | bytes 6258688 | tf_op jit(solution)/shard_map/dot_general | solution.py:208
  176.6 3.0 %fusion.15 = bf16[1,2048,384]{2,1,0:T(8,128)(2,1)} fusion(bf16[2048,384]{1,0:T(8,128)(2,1)S(1)} %collective-permute-done.3, bf16[80,8,16,128]{3,2,1,0:T(8,128)(2,1)S(1)} %bitcast.44, bf16[640,768]{1,0:T(8,128)(2,1)S(1)} %copy-done.4), kind=kOutput, calls=%fused_computation.18 | convolution fusion | flops 1008992256 | bytes 6258688 | tf_op jit(solution)/shard_map/dot_general | solution.py:208
  179.7 3.0 %fusion.18 = bf16[1,2048,384]{2,1,0:T(8,128)(2,1)} fusion(bf16[2048,384]{1,0:T(8,128)(2,1)S(1)} %collective-permute-done.4, bf16[80,8,16,128]{3,2,1,0:T(8,128)(2,1)S(1)} %bitcast.45, bf16[640,768]{1,0:T(8,128)(2,1)S(1)} %copy-done.3), kind=kOutput, calls=%fused_computation.19 | convolution fusion | flops 1008992256 | bytes 6258688 | tf_op jit(solution)/shard_map/dot_general | solution.py:208
  182.7 45.9 %all-to-all-done.1.rows = bf16[640,16,128]{2,1,0:T(8,128)(2,1)S(1)} async-done(((bf16[640,16,128]{2,1,0:T(8,128)(2,1)}), bf16[640,16,128]{2,1,0:T(8,128)(2,1)S(1)}, u32[]{:S(2)}, u32[]{:S(2)}) %all-to-all-start.1) | async-done | bytes 2621472 | tf_op jit(solution)/shard_map/all_to_all | solution.py:216
  228.6 2.4 %combine.1 = bf16[128,2048]{1,0:T(8,128)(2,1)} custom-call(s32[4,128]{1,0:T(4,128)S(1)} %copy-done, bf16[640,16,128]{2,1,0:T(8,128)(2,1)S(1)} %all-to-all-done.1.rows), custom_call_target="tpu_custom_call" | custom-call | tf_op jit(solution)/shard_map/combine/pallas_call | solution.py:196
  (15 shorter events, 0.0 us)
Async XLA Ops:
  6.0 15.6 %copy-start.1 = (bf16[1,2048,384]{2,1,0:T(8,128)(2,1)S(1)}, bf16[1,2048,384]{2,1,0:T(8,128)(2,1)}, u32[]{:S(2)}) copy-start(bf16[1,2048,384]{2,1,0:T(8,128)(2,1)} %param.11) | copy-start | bytes 4718596
  6.0 133.9 %all-to-all-start = ((bf16[1280,16,128]{2,1,0:T(8,128)(2,1)}), bf16[1280,16,128]{2,1,0:T(8,128)(2,1)}, u32[]{:S(2)}, u32[]{:S(2)}) async-start(bf16[1280,16,128]{2,1,0:T(8,128)(2,1)} %get-tuple-element.11), calls=%async_computation | async-start | bytes 10485760 | tf_op jit(solution)/shard_map/all_to_all | solution.py:216
  21.5 4.7 %collective-permute-start = (bf16[2048,384]{1,0:T(8,128)(2,1)S(1)}, bf16[2048,384]{1,0:T(8,128)(2,1)S(1)}, u32[]{:S(2)}, u32[]{:S(2)}) collective-permute-start(bf16[2048,384]{1,0:T(8,128)(2,1)S(1)} %bitcast.49), channel_id=1, source_target_pairs={{0,128},{128,0},{1,129},{129,1},{2,130},{130,2},{3,131},{131,3},{4... | collective-permute-start | bytes 4718600 | tf_op jit(solution)/shard_map/ppermute | solution.py:215
  21.6 6.3 %collective-permute-start.1 = (bf16[2048,384]{1,0:T(8,128)(2,1)}, bf16[2048,384]{1,0:T(8,128)(2,1)S(1)}, u32[]{:S(2)}, u32[]{:S(2)}) collective-permute-start(bf16[2048,384]{1,0:T(8,128)(2,1)} %bitcast.4), channel_id=1, source_target_pairs={{0,128},{128,0},{1,129},{129,1},{2,130},{130,2},{3,131},{131,3},{4... | collective-permute-start | bytes 4718600 | tf_op jit(solution)/shard_map/ppermute | solution.py:215
  22.1 9.2 %collective-permute-start.2 = (bf16[384,2048]{1,0:T(8,128)(2,1)}, bf16[384,2048]{1,0:T(8,128)(2,1)S(1)}, u32[]{:S(2)}, u32[]{:S(2)}) collective-permute-start(bf16[384,2048]{1,0:T(8,128)(2,1)} %bitcast.5), channel_id=1, source_target_pairs={{0,128},{128,0},{1,129},{129,1},{2,130},{130,2},{3,131},{131,3},{4... | collective-permute-start | bytes 4718600 | tf_op jit(solution)/shard_map/ppermute | solution.py:215
  155.8 72.8 %all-to-all-start.1 = ((bf16[640,16,128]{2,1,0:T(8,128)(2,1)}), bf16[640,16,128]{2,1,0:T(8,128)(2,1)S(1)}, u32[]{:S(2)}, u32[]{:S(2)}) async-start(bf16[640,16,128]{2,1,0:T(8,128)(2,1)} %get-tuple-element.12), calls=%async_computation.1 | async-start | bytes 5242880 | tf_op jit(solution)/shard_map/all_to_all | solution.py:216
  164.3 3.6 %copy-start.2 = (bf16[640,768]{1,0:T(8,128)(2,1)S(1)}, bf16[640,768]{1,0:T(8,128)(2,1)}, u32[]{:S(2)}) copy-start(bf16[640,768]{1,0:T(8,128)(2,1)} %get-tuple-element.15) | copy-start | bytes 2949124
  167.9 1.6 copy-start.4
  169.3 4.7 %collective-permute-start.5 = (bf16[384,2048]{1,0:T(8,128)(2,1)S(1)}, bf16[384,2048]{1,0:T(8,128)(2,1)S(1)}, u32[]{:S(2)}, u32[]{:S(2)}) collective-permute-start(bf16[384,2048]{1,0:T(8,128)(2,1)S(1)} %convolution_convert_fusion), channel_id=1, source_target_pairs={{0,128},{128,0},{1,129},{129,1},{2,130},{130,2},{3,131},{131,3},{4... | collective-permute-start | bytes 4718600 | tf_op jit(solution)/shard_map/ppermute | solution.py:215
  169.4 2.4 %copy-start.3 = (bf16[640,768]{1,0:T(8,128)(2,1)S(1)}, bf16[640,768]{1,0:T(8,128)(2,1)}, u32[]{:S(2)}) copy-start(bf16[640,768]{1,0:T(8,128)(2,1)} %get-tuple-element.14) | copy-start | bytes 2949124
  171.2 5.4 %collective-permute-start.3 = (bf16[2048,384]{1,0:T(8,128)(2,1)S(1)}, bf16[2048,384]{1,0:T(8,128)(2,1)S(1)}, u32[]{:S(2)}, u32[]{:S(2)}) collective-permute-start(bf16[2048,384]{1,0:T(8,128)(2,1)S(1)} %convolution_convert_fusion.2), channel_id=1, source_target_pairs={{0,128},{128,0},{1,129},{129,1},{2,130},{130,2},{3,131},{131,3},{4... | collective-permute-start | bytes 4718600 | tf_op jit(solution)/shard_map/ppermute | solution.py:215
  173.6 6.1 %collective-permute-start.4 = (bf16[2048,384]{1,0:T(8,128)(2,1)S(1)}, bf16[2048,384]{1,0:T(8,128)(2,1)S(1)}, u32[]{:S(2)}, u32[]{:S(2)}) collective-permute-start(bf16[2048,384]{1,0:T(8,128)(2,1)S(1)} %convolution_convert_fusion.1), channel_id=1, source_target_pairs={{0,128},{128,0},{1,129},{129,1},{2,130},{130,2},{3,131},{131,3},{4... | collective-permute-start | bytes 4718600 | tf_op jit(solution)/shard_map/ppermute | solution.py:215
  179.7 48.9 %copy-start = (s32[4,128]{1,0:T(4,128)S(1)}, s32[4,128]{1,0:T(4,128)}, u32[]{:S(2)}) copy-start(s32[4,128]{1,0:T(4,128)} %get-tuple-element.10.place) | copy-start | bytes 6148

commit v7 on v6

--- a/solution.py
+++ b/solution.py
@@ -180,7 +180,7 @@
     ))
 
 
-def combine_kernel(place, rows, out, sums):
+def combine_kernel(chunks, place, rows, out, sums, v_out, sems):
     def one_token(t, carry):
         total = rows[place[0, t]].astype(jnp.float32)
         for k in range(1, place.shape[0]):
@@ -188,17 +188,29 @@
         sums[t] = total.astype(jnp.bfloat16)
         return carry
 
-    lax.fori_loop(0, out.shape[0], one_token, 0, unroll=8)
-    out[...] = sums[...].reshape(out.shape)
-
-
-def combine(place, rows, tokens, width):
+    some, width = out.shape[0] // chunks, out.shape[1]
+    done = []
+    for i in range(chunks):
+        lax.fori_loop(i * some, (i + 1) * some, one_token, 0, unroll=8)
+        r = pl.ds(i * some, some)
+        v_out[r, :] = sums[r].reshape(some, width)
+        done.append(pltpu.make_async_copy(v_out.at[r], out.at[r], sems.at[i]))
+        done[-1].start()
+    for d in done:
+        d.wait()
+
+
+def combine(place, rows, tokens, width, chunks=4):
     return pl.pallas_call(
-        combine_kernel,
+        functools.partial(combine_kernel, chunks),
         out_shape=jax.ShapeDtypeStruct((tokens, width), jnp.bfloat16),
         in_specs=[SMEM, VMEM],
-        out_specs=VMEM,
-        scratch_shapes=[pltpu.VMEM((tokens,) + rows.shape[1:], jnp.bfloat16)],
+        out_specs=ANY,
+        scratch_shapes=[
+            pltpu.VMEM((tokens,) + rows.shape[1:], jnp.bfloat16),
+            pltpu.VMEM((tokens, width), jnp.bfloat16),
+            pltpu.SemaphoreType.DMA((chunks,)),
+        ],
         compiler_params=pltpu.CompilerParams(vmem_limit_bytes=16 * 2**20),
         name="combine",
     )(place, rows)

time: 231 us -> 231 us (level)
  no operation moved by 1% of the time
where the time goes in v7:
time: 231 us
  waiting for transfers between devices  155 us (67%)
  starting transfers between devices  25.8 us (11%)
  Pallas kernels  23.5 us (10%)
  matrix products  13.7 us (6%)
  other arithmetic  8.49 us (4%)
  local copies, waits for them, and re-layouts  3.57 us (2%)
    all_to_all x2, waiting for transfers between devices, local(): lax.all_to_all(a, 'ep', split_axis=0, concat_axis=0, tiled=True)  151 us
    all_to_all x2, starting transfers between devices, local(): lax.all_to_all(a, 'ep', split_axis=0, concat_axis=0, tiled=True)  24.1 us
    pallas_call x1, Pallas kernels, row_grads(): pl.pallas_call(functools.partial(row_grads_kernel, parts, columns), out_s...  15.9 us
    dot_general x6, matrix products, contract(): lax.dot_general(left, right, (dims, ((), ())), preferred_element_type=jnp...  13.7 us
    concatenate x3, other arithmetic, local(): jnp.concatenate([w[0], swap(w[0])], axis=axis)  8.49 us
    pallas_call x1, Pallas kernels, fill_slots(): pl.pallas_call(functools.partial(fill_kernel, chunks), out_shape=(jax.Sha...  5.31 us
  transfers between devices with their start and end apart: 8, of which 3 were waited for; matrix products, arithmetic and copies ran while one was open for 11% of the time, Pallas kernels for 0%

profile of v7, /device:TPU:32, one launch (start us, length us, event | category | flops | bytes accessed | tf_op | source)
XLA Modules:
  0.0 231.1 jit_solution(17099875966545351717)
XLA Ops:
  0.6 5.3 %fill_slots.1 = (bf16[1280,16,128]{2,1,0:T(8,128)(2,1)}, s32[4,128]{1,0:T(4,128)}) custom-call(s32[4,128]{1,0:T(4,128)} %bitcast.50, bf16[4,128]{1,0:T(4,128)(2,1)} %bitcast.51, bf16[128,2048]{1,0:T(8,128)(2,1)} %x.1, bf16[128,2048]{1,0:T(8,128)(2,1)} %dy.1), custom_call_target="tpu_custom_call" | custom-call | tf_op jit(solution)/shard_map/fill_slots/pallas_call | solution.py:84
  6.0 15.6 %all-to-all-start = ((bf16[1280,16,128]{2,1,0:T(8,128)(2,1)}), bf16[1280,16,128]{2,1,0:T(8,128)(2,1)}, u32[]{:S(2)}, u32[]{:S(2)}) async-start(bf16[1280,16,128]{2,1,0:T(8,128)(2,1)} %get-tuple-element.11), calls=%async_computation | async-start | bytes 10485760 | tf_op jit(solution)/shard_map/all_to_all | solution.py:228
  21.5 0.1 collective-permute-start
  21.6 0.5 collective-permute-start.1
  22.1 0.1 collective-permute-start.2
  22.2 4.0 %collective-permute-done = bf16[2048,384]{1,0:T(8,128)(2,1)S(1)} collective-permute-done((bf16[2048,384]{1,0:T(8,128)(2,1)S(1)}, bf16[2048,384]{1,0:T(8,128)(2,1)S(1)}, u32[]{:S(2)}, u32[]{:S(2)}) %collective-permute-start) | collective-permute-done | bytes 1572896 | tf_op jit(solution)/shard_map/ppermute | solution.py:227
  26.3 1.7 pad_maximum_fusion.w_gate
  27.9 3.4 %pad_maximum_fusion.1.up = bf16[2048,768]{1,0:T(8,128)(2,1)} fusion(bf16[2048,384]{1,0:T(8,128)(2,1)S(1)} %collective-permute-done.1, bf16[2048,384]{1,0:T(8,128)(2,1)} %bitcast.4), kind=kLoop, calls=%fused_computation.1 | loop fusion | flops 6291456 | bytes 6291456 | tf_op jit(solution)/shard_map/concatenate | solution.py:234
  31.4 3.4 %pad_maximum_fusion.2.down = bf16[768,2048]{1,0:T(8,128)(2,1)} fusion(bf16[384,2048]{1,0:T(8,128)(2,1)S(1)} %collective-permute-done.2, bf16[384,2048]{1,0:T(8,128)(2,1)} %bitcast.5), kind=kLoop, calls=%fused_computation.2 | loop fusion | flops 6291456 | bytes 6291456 | tf_op jit(solution)/shard_map/concatenate | solution.py:234
  34.8 105.1 %all-to-all-done = bf16[1280,16,128]{2,1,0:T(8,128)(2,1)} async-done(((bf16[1280,16,128]{2,1,0:T(8,128)(2,1)}), bf16[1280,16,128]{2,1,0:T(8,128)(2,1)}, u32[]{:S(2)}, u32[]{:S(2)}) %all-to-all-start) | async-done | bytes 5242912 | tf_op jit(solution)/shard_map/all_to_all | solution.py:228
  139.9 15.9 %row_grads.1 = (bf16[640,16,128]{2,1,0:T(8,128)(2,1)}, bf16[640,768]{1,0:T(8,128)(2,1)}, bf16[640,768]{1,0:T(8,128)(2,1)}, bf16[640,768]{1,0:T(8,128)(2,1)}) custom-call(bf16[128,10,16,128]{3,2,1,0:T(8,128)(2,1)} %bitcast.2.arrived, bf16[2048,768]{1,0:T(8,128)(2,1)S(1)} %pad_maximum_fusion.w_gate, bf16[2048,768]{1,0:T(8,128)(2,1)} %pad_maximum_fusion.1.up, ...), custom_call_target="tpu_custom_call" | custom-call | flops 10066329600 | bytes 25165824 | tf_op jit(solution)/shard_map/row_grads/pallas_call | solution.py:161
  155.8 8.5 %all-to-all-start.1 = ((bf16[640,16,128]{2,1,0:T(8,128)(2,1)}), bf16[640,16,128]{2,1,0:T(8,128)(2,1)S(1)}, u32[]{:S(2)}, u32[]{:S(2)}) async-start(bf16[640,16,128]{2,1,0:T(8,128)(2,1)} %get-tuple-element.12), calls=%async_computation.1 | async-start | bytes 5242880 | tf_op jit(solution)/shard_map/all_to_all | solution.py:228
  164.3 3.5 %fusion.36 = (bf16[128,5,16,128]{3,2,1,0:T(8,128)(2,1)S(1)}, bf16[128,5,16,128]{3,2,1,0:T(8,128)(2,1)S(1)}) fusion(bf16[128,10,16,128]{3,2,1,0:T(8,128)(2,1)} %bitcast.2.arrived), kind=kLoop, calls=%fused_computation.33 | loop fusion | bytes 10485760 | tf_op jit(solution)/shard_map/slice | solution.py:242
  167.9 1.4 convolution_convert_fusion
  169.3 0.1 collective-permute-start.5
  169.4 1.8 convolution_convert_fusion.2
  171.2 0.6 collective-permute-start.3
  171.8 1.8 convolution_convert_fusion.1
  173.6 0.4 collective-permute-start.4
  174.0 2.6 %fusion.21 = bf16[1,384,2048]{2,1,0:T(8,128)(2,1)} fusion(bf16[384,2048]{1,0:T(8,128)(2,1)S(1)} %collective-permute-done.5, bf16[80,8,16,128]{3,2,1,0:T(8,128)(2,1)S(1)} %bitcast.47, bf16[640,768]{1,0:T(8,128)(2,1)S(1)} %copy-done.2), kind=kOutput, calls=%fused_computation.20 | convolution fusion | flops 1008992256 | bytes 6258688 | tf_op jit(solution)/shard_map/dot_general | solution.py:220
  176.6 3.0 %fusion.15 = bf16[1,2048,384]{2,1,0:T(8,128)(2,1)} fusion(bf16[2048,384]{1,0:T(8,128)(2,1)S(1)} %collective-permute-done.3, bf16[80,8,16,128]{3,2,1,0:T(8,128)(2,1)S(1)} %bitcast.44, bf16[640,768]{1,0:T(8,128)(2,1)S(1)} %copy-done.4), kind=kOutput, calls=%fused_computation.18 | convolution fusion | flops 1008992256 | bytes 6258688 | tf_op jit(solution)/shard_map/dot_general | solution.py:220
  179.7 3.0 %fusion.18 = bf16[1,2048,384]{2,1,0:T(8,128)(2,1)} fusion(bf16[2048,384]{1,0:T(8,128)(2,1)S(1)} %collective-permute-done.4, bf16[80,8,16,128]{3,2,1,0:T(8,128)(2,1)S(1)} %bitcast.45, bf16[640,768]{1,0:T(8,128)(2,1)S(1)} %copy-done.3), kind=kOutput, calls=%fused_computation.19 | convolution fusion | flops 1008992256 | bytes 6258688 | tf_op jit(solution)/shard_map/dot_general | solution.py:220
  182.7 45.9 %all-to-all-done.1.rows = bf16[640,16,128]{2,1,0:T(8,128)(2,1)S(1)} async-done(((bf16[640,16,128]{2,1,0:T(8,128)(2,1)}), bf16[640,16,128]{2,1,0:T(8,128)(2,1)S(1)}, u32[]{:S(2)}, u32[]{:S(2)}) %all-to-all-start.1) | async-done | bytes 2621472 | tf_op jit(solution)/shard_map/all_to_all | solution.py:228
  228.6 2.3 %combine.1 = bf16[128,2048]{1,0:T(8,128)(2,1)} custom-call(s32[4,128]{1,0:T(4,128)S(1)} %copy-done, bf16[640,16,128]{2,1,0:T(8,128)(2,1)S(1)} %all-to-all-done.1.rows), custom_call_target="tpu_custom_call" | custom-call | tf_op jit(solution)/shard_map/combine/pallas_call | solution.py:204
  (15 shorter events, 0.0 us)
Async XLA Ops:
  6.0 15.6 %copy-start.1 = (bf16[1,2048,384]{2,1,0:T(8,128)(2,1)S(1)}, bf16[1,2048,384]{2,1,0:T(8,128)(2,1)}, u32[]{:S(2)}) copy-start(bf16[1,2048,384]{2,1,0:T(8,128)(2,1)} %param.11) | copy-start | bytes 4718596
  6.0 133.9 %all-to-all-start = ((bf16[1280,16,128]{2,1,0:T(8,128)(2,1)}), bf16[1280,16,128]{2,1,0:T(8,128)(2,1)}, u32[]{:S(2)}, u32[]{:S(2)}) async-start(bf16[1280,16,128]{2,1,0:T(8,128)(2,1)} %get-tuple-element.11), calls=%async_computation | async-start | bytes 10485760 | tf_op jit(solution)/shard_map/all_to_all | solution.py:228
  21.5 4.7 %collective-permute-start = (bf16[2048,384]{1,0:T(8,128)(2,1)S(1)}, bf16[2048,384]{1,0:T(8,128)(2,1)S(1)}, u32[]{:S(2)}, u32[]{:S(2)}) collective-permute-start(bf16[2048,384]{1,0:T(8,128)(2,1)S(1)} %bitcast.49), channel_id=1, source_target_pairs={{0,128},{128,0},{1,129},{129,1},{2,130},{130,2},{3,131},{131,3},{4... | collective-permute-start | bytes 4718600 | tf_op jit(solution)/shard_map/ppermute | solution.py:227
  21.6 6.3 %collective-permute-start.1 = (bf16[2048,384]{1,0:T(8,128)(2,1)}, bf16[2048,384]{1,0:T(8,128)(2,1)S(1)}, u32[]{:S(2)}, u32[]{:S(2)}) collective-permute-start(bf16[2048,384]{1,0:T(8,128)(2,1)} %bitcast.4), channel_id=1, source_target_pairs={{0,128},{128,0},{1,129},{129,1},{2,130},{130,2},{3,131},{131,3},{4... | collective-permute-start | bytes 4718600 | tf_op jit(solution)/shard_map/ppermute | solution.py:227
  22.1 9.2 %collective-permute-start.2 = (bf16[384,2048]{1,0:T(8,128)(2,1)}, bf16[384,2048]{1,0:T(8,128)(2,1)S(1)}, u32[]{:S(2)}, u32[]{:S(2)}) collective-permute-start(bf16[384,2048]{1,0:T(8,128)(2,1)} %bitcast.5), channel_id=1, source_target_pairs={{0,128},{128,0},{1,129},{129,1},{2,130},{130,2},{3,131},{131,3},{4... | collective-permute-start | bytes 4718600 | tf_op jit(solution)/shard_map/ppermute | solution.py:227
  155.8 72.8 %all-to-all-start.1 = ((bf16[640,16,128]{2,1,0:T(8,128)(2,1)}), bf16[640,16,128]{2,1,0:T(8,128)(2,1)S(1)}, u32[]{:S(2)}, u32[]{:S(2)}) async-start(bf16[640,16,128]{2,1,0:T(8,128)(2,1)} %get-tuple-element.12), calls=%async_computation.1 | async-start | bytes 5242880 | tf_op jit(solution)/shard_map/all_to_all | solution.py:228
  164.3 3.6 %copy-start.2 = (bf16[640,768]{1,0:T(8,128)(2,1)S(1)}, bf16[640,768]{1,0:T(8,128)(2,1)}, u32[]{:S(2)}) copy-start(bf16[640,768]{1,0:T(8,128)(2,1)} %get-tuple-element.15) | copy-start | bytes 2949124
  167.9 1.6 copy-start.4
  169.3 4.7 %collective-permute-start.5 = (bf16[384,2048]{1,0:T(8,128)(2,1)S(1)}, bf16[384,2048]{1,0:T(8,128)(2,1)S(1)}, u32[]{:S(2)}, u32[]{:S(2)}) collective-permute-start(bf16[384,2048]{1,0:T(8,128)(2,1)S(1)} %convolution_convert_fusion), channel_id=1, source_target_pairs={{0,128},{128,0},{1,129},{129,1},{2,130},{130,2},{3,131},{131,3},{4... | collective-permute-start | bytes 4718600 | tf_op jit(solution)/shard_map/ppermute | solution.py:227
  169.4 2.4 %copy-start.3 = (bf16[640,768]{1,0:T(8,128)(2,1)S(1)}, bf16[640,768]{1,0:T(8,128)(2,1)}, u32[]{:S(2)}) copy-start(bf16[640,768]{1,0:T(8,128)(2,1)} %get-tuple-element.14) | copy-start | bytes 2949124
  171.2 5.4 %collective-permute-start.3 = (bf16[2048,384]{1,0:T(8,128)(2,1)S(1)}, bf16[2048,384]{1,0:T(8,128)(2,1)S(1)}, u32[]{:S(2)}, u32[]{:S(2)}) collective-permute-start(bf16[2048,384]{1,0:T(8,128)(2,1)S(1)} %convolution_convert_fusion.2), channel_id=1, source_target_pairs={{0,128},{128,0},{1,129},{129,1},{2,130},{130,2},{3,131},{131,3},{4... | collective-permute-start | bytes 4718600 | tf_op jit(solution)/shard_map/ppermute | solution.py:227
  173.6 6.1 %collective-permute-start.4 = (bf16[2048,384]{1,0:T(8,128)(2,1)S(1)}, bf16[2048,384]{1,0:T(8,128)(2,1)S(1)}, u32[]{:S(2)}, u32[]{:S(2)}) collective-permute-start(bf16[2048,384]{1,0:T(8,128)(2,1)S(1)} %convolution_convert_fusion.1), channel_id=1, source_target_pairs={{0,128},{128,0},{1,129},{129,1},{2,130},{130,2},{3,131},{131,3},{4... | collective-permute-start | bytes 4718600 | tf_op jit(solution)/shard_map/ppermute | solution.py:227
  179.7 48.9 %copy-start = (s32[4,128]{1,0:T(4,128)S(1)}, s32[4,128]{1,0:T(4,128)}, u32[]{:S(2)}) copy-start(s32[4,128]{1,0:T(4,128)} %get-tuple-element.10.place) | copy-start | bytes 6148
